TPU v7x, 256 devices: a whole 4x4x8 slice. The times are simulated.
256 devices in a mesh: lon: 64 (over y_lo, z, x), lat: 2 (over y_hi), head: 2 (over core).
Axes of the slice: x: 4, y: 4 (y_hi: 2, y_lo: 2; y = y_hi * 2 + y_lo), z: 8, core: 2. Of those that a mesh axis runs over, the one named last changes fastest.
Arguments:
- tokens: bfloat16 [2, 24, 384, 1024], P(None, 'lat', 'lon', 'head')
- grad_out: bfloat16 [2, 24, 384, 1024], P(None, 'lat', 'lon', 'head'), may hold values from -16 to 16
- w_qkv: bfloat16 [3, 1024, 1024], P(None, None, 'head')
- w_out: bfloat16 [1024, 1024], P('head'), may hold values from -0.1875 to 0.1875
- band_count: int32 [24], replicated, may hold values from 96 to 384
- lat_shift: int32 [1], replicated, may hold values from 1 to 11
- lon_shift: int32 [1], replicated, may hold values from 1 to 5
Outputs:
- grad_tokens: bfloat16 [2, 24, 384, 1024], P(None, 'lat', 'lon', 'head')
- grad_qkv: float32 [3, 1024, 1024], P(None, ('lon', 'lat'), 'head')
All inputs are finite; a program needn't handle non-finite values.
Results may differ from a plain program's by a relative error of at most 0.012.
The roundings to bfloat16 on the way count: a program that leaves them out, or rounds other values in their place, can miss the bound.
Values may be sent and summed in bfloat16 or wider, within the bound.
A program may use at most 448 MiB of HBM per device.

v0:
```python
import jax
import jax.numpy as jnp
from jax import lax
from jax.sharding import PartitionSpec as P

HEAD_DIM = 64
WLAT = 12
WLON = 6


def from_behind(block, axis, distance):
    devices = range(lax.axis_size(axis))
    route = [((i - distance) % len(devices), i) for i in devices]
    return lax.ppermute(block, axis, route)


def widen(paired):
    return lax.all_gather(paired, "head", axis=4, tiled=True)


def extend(paired):
    strips = from_behind(paired, "lon", -1)
    paired = jnp.concatenate([paired, strips], 3)
    rims = from_behind(paired, "lat", -1)
    return jnp.concatenate([paired, rims], 2)


def head_sum(grid):
    return lax.psum_scatter(grid, "head", scatter_dimension=3, tiled=True)


def give_back(grid, block_rows, block_cols):
    returned = from_behind(grid[:, block_rows:].astype(jnp.bfloat16), "lat", 1).astype(jnp.float32)
    grid = jnp.concatenate([grid[:, :WLAT] + returned, grid[:, WLAT:block_rows]], 1)
    side_cols = from_behind(grid[:, :, block_cols:], "lon", 1)
    return jnp.concatenate([grid[:, :, :WLON] + side_cols, grid[:, :, WLON:block_cols]], 2)


def to_windows(array, levels, block_rows, block_cols):
    features = array.shape[-1]
    shaped = array.reshape(levels, block_rows // WLAT, WLAT, block_cols // WLON, WLON, features)
    return shaped.transpose(1, 3, 0, 2, 4, 5).reshape(-1, levels * WLAT * WLON, features)


def from_windows(array, levels, block_rows, block_cols):
    features = array.shape[-1]
    shaped = array.reshape(block_rows // WLAT, block_cols // WLON, levels, WLAT, WLON, features)
    return shaped.transpose(2, 0, 3, 1, 4, 5).reshape(levels, block_rows, block_cols, features)


def shards(tokens, grad_out, w_qkv, w_out, band_count, lat_shift, lon_shift):
    levels, block_rows, block_cols, half_width = tokens.shape
    paired = jnp.stack([tokens, grad_out])
    paired = extend(widen(paired))
    model_width = paired.shape[4]
    row_shift = lat_shift[0]
    col_shift = lon_shift[0]
    shifted = lax.dynamic_slice(
        paired, (0, 0, row_shift, col_shift, 0), (2, levels, block_rows, block_cols, model_width)
    )
    grid_rows = block_rows * lax.axis_size("lat")
    grid_cols = block_cols * lax.axis_size("lon")
    raw_rows = (
        lax.axis_index("lat") * block_rows + row_shift + jnp.arange(block_rows, dtype=jnp.int32)
    )
    glob_rows = raw_rows % grid_rows
    glob_cols = (
        lax.axis_index("lon") * block_cols + col_shift + jnp.arange(block_cols, dtype=jnp.int32)
    ) % grid_cols
    row_match = glob_rows[:, None] == jnp.arange(grid_rows, dtype=jnp.int32)[None, :]
    row_counts = jnp.sum(jnp.where(row_match, band_count[None, :], 0), axis=1)
    is_valid = glob_cols[None, :] < row_counts[:, None]
    seam_side = jnp.broadcast_to((raw_rows >= grid_rows)[:, None], (block_rows, block_cols))
    masks = jnp.stack([is_valid, seam_side], -1).astype(jnp.int32)
    masks = jnp.broadcast_to(masks[None], (levels, block_rows, block_cols, 2))
    mask_windows = to_windows(masks, levels, block_rows, block_cols)
    valid_keys = mask_windows[..., 0] > 0
    side_windows = mask_windows[..., 1]
    in_windows = to_windows(shifted[0], levels, block_rows, block_cols)
    windows, window, _ = in_windows.shape
    flat_in = in_windows.reshape(-1, model_width)
    flat_grad = to_windows(shifted[1], levels, block_rows, block_cols).reshape(-1, model_width)
    query = jnp.dot(flat_in, w_qkv[0], preferred_element_type=jnp.float32).astype(jnp.bfloat16)
    keys = jnp.dot(flat_in, w_qkv[1], preferred_element_type=jnp.float32).astype(jnp.bfloat16)
    values = jnp.dot(flat_in, w_qkv[2], preferred_element_type=jnp.float32).astype(jnp.bfloat16)
    head_count = half_width // HEAD_DIM
    score_scale = HEAD_DIM ** (-0.5)

    def per_head(array):
        return array.reshape(windows, window, head_count, HEAD_DIM)

    scores = (
        jnp.einsum(
            "pqhe,pkhe->phqk", per_head(query), per_head(keys), preferred_element_type=jnp.float32
        )
        * score_scale
    )
    itself = jnp.eye(window, dtype=bool)
    allowed = (valid_keys[:, None, :] | itself[None]) & (
        side_windows[:, :, None] == side_windows[:, None, :]
    )
    scores = jnp.where(allowed[:, None], scores, jnp.float32(-1e30))
    highest = jnp.max(scores, -1, keepdims=True)
    raised = jnp.exp(scores - highest)
    attn_probs = raised / jnp.sum(raised, -1, keepdims=True)
    probs_b = attn_probs.astype(jnp.bfloat16)
    grad_attended = jnp.einsum(
        "td,cd->tc", flat_grad, w_out, preferred_element_type=jnp.float32
    ).astype(jnp.bfloat16)
    grad_heads = per_head(grad_attended)
    grad_values = (
        jnp.einsum("phqk,pqhe->pkhe", probs_b, grad_heads, preferred_element_type=jnp.float32)
        .astype(jnp.bfloat16)
        .reshape(-1, half_width)
    )
    grad_probs = jnp.einsum(
        "pqhe,pkhe->phqk", grad_heads, per_head(values), preferred_element_type=jnp.float32
    )
    inner = jnp.sum(attn_probs * grad_probs, -1, keepdims=True)
    grad_scores = (attn_probs * (grad_probs - inner) * score_scale).astype(jnp.bfloat16)
    grad_query = (
        jnp.einsum(
            "phqk,pkhe->pqhe", grad_scores, per_head(keys), preferred_element_type=jnp.float32
        )
        .astype(jnp.bfloat16)
        .reshape(-1, half_width)
    )
    grad_keys = (
        jnp.einsum(
            "phqk,pqhe->pkhe", grad_scores, per_head(query), preferred_element_type=jnp.float32
        )
        .astype(jnp.bfloat16)
        .reshape(-1, half_width)
    )
    grad_in = jnp.einsum("tc,dc->td", grad_query, w_qkv[0], preferred_element_type=jnp.float32)
    grad_in = grad_in + jnp.einsum(
        "tc,dc->td", grad_keys, w_qkv[1], preferred_element_type=jnp.float32
    )
    grad_in = grad_in + jnp.einsum(
        "tc,dc->td", grad_values, w_qkv[2], preferred_element_type=jnp.float32
    )
    grad_cat = jnp.concatenate([grad_query, grad_keys, grad_values], 1)
    row_total = model_width // (lax.axis_size("lon") * lax.axis_size("lat"))
    summed = lax.psum_scatter(
        jnp.einsum("td,tc->dc", flat_in, grad_cat, preferred_element_type=jnp.float32),
        ("lon", "lat"),
        scatter_dimension=0,
        tiled=True,
    )
    grad_qkv = summed.reshape(row_total, 3, half_width).transpose(1, 0, 2)
    grid = from_windows(
        grad_in.reshape(windows, window, model_width), levels, block_rows, block_cols
    )
    extended_zero = jnp.zeros(
        (levels, block_rows + WLAT, block_cols + WLON, model_width), jnp.float32
    )
    extended_grid = lax.dynamic_update_slice(extended_zero, grid, (0, row_shift, col_shift, 0))
    total = head_sum(give_back(extended_grid, block_rows, block_cols))
    return (total.astype(jnp.bfloat16), grad_qkv)


def solution(mesh):
    in_specs = (
        P(None, "lat", "lon", "head"),
        P(None, "lat", "lon", "head"),
        P(None, None, "head"),
        P("head", None),
        P(),
        P(),
        P(),
    )
    out_specs = (P(None, "lat", "lon", "head"), P(None, ("lon", "lat"), "head"))
    return jax.shard_map(shards, mesh=mesh, in_specs=in_specs, out_specs=out_specs, check_vma=False)
```

profile of v0, /device:TPU:128, one launch (start us, length us, event | category | flops | bytes accessed | tf_op | source)
XLA Modules:
  0.0 929.4 jit_solution(2118006250138920653)
XLA Ops:
  8.7 2.2 all_gather.3
  11.0 2.3 collective-permute-start
  13.9 12.5 %collective-permute-done = bf16[2,2,12,6,1024]{4,1,3,2,0:T(2,128)(2,1)S(1)} collective-permute-done((bf16[2,2,12,6,1024]{4,1,3,2,0:T(2,128)(2,1)S(1)}, bf16[2,2,12,6,1024]{4,1,3,2,0:T(2,128)(2,1)S(1)}, u32[]{:S(2)}, u32[]{:S(2)}) %collective-permute-start) | collective-permute-done | bytes 589856 | tf_op jit(solution)/shard_map/ppermute | solution.py:14
  26.8 3.3 collective-permute-start.1
  32.1 23.5 %collective-permute-done.1 = bf16[2,2,12,12,1024]{4,1,3,2,0:T(2,128)(2,1)S(1)} collective-permute-done((bf16[2,2,12,12,1024]{4,1,3,2,0:T(2,128)(2,1)S(1)}, bf16[2,2,12,12,1024]{4,1,3,2,0:T(2,128)(2,1)S(1)}, u32[]{:S(2)}, u32[]{:S(2)}) %collective-permute-start.1) | collective-permute-done | bytes 1179680 | tf_op jit(solution)/shard_map/ppermute | solution.py:14
  60.8 1.6 convolution_convert_fusion.6
  64.0 1.6 fusion.49
  65.6 1.6 convolution_convert_fusion
  67.2 2.1 convolution_convert_fusion.1
  69.3 2.1 convolution_convert_fusion.2
  71.4 1.8 fusion.16
  73.2 1.7 convolution_add_fusion.1
  75.0 1.7 convolution_add_fusion
  78.8 3.4 collective-permute-start.2
  82.2 11.9 %collective-permute-done.2 = bf16[2,12,12,1024]{3,0,2,1:T(2,128)(2,1)S(1)} collective-permute-done((bf16[2,12,12,1024]{3,0,2,1:T(2,128)(2,1)S(1)}, bf16[2,12,12,1024]{3,0,2,1:T(2,128)(2,1)S(1)}, u32[]{:S(2)}, u32[]{:S(2)}) %collective-permute-start.2) | collective-permute-done | bytes 589856 | tf_op jit(solution)/shard_map/ppermute | solution.py:14
  94.9 1.6 collective-permute-start.3
  96.4 15.1 %collective-permute-done.3 = f32[2,12,6,1024]{3,0,2,1:T(2,128)S(1)} collective-permute-done((f32[2,12,6,1024]{3,0,2,1:T(2,128)S(1)}, f32[2,12,6,1024]{3,0,2,1:T(2,128)S(1)}, u32[]{:S(2)}, u32[]{:S(2)}) %collective-permute-start.3) | collective-permute-done | bytes 589856 | tf_op jit(solution)/shard_map/ppermute | solution.py:14
  112.1 38.4 %copy.63 = f32[2,12,6,1024]{0,2,1,3:T(8,128)} copy(f32[2,12,6,1024]{3,0,2,1:T(2,128)S(1)} %slice_add_fusion.1) | data formatting | bytes 1179648
  150.5 29.7 %reshape.265 = f32[1024,144]{1,0:T(8,128)} reshape(f32[1024,12,6,2]{3,2,1,0:T(8,128)} %bitcast.71) | data formatting | bytes 1179648
  181.2 3.7 fusion.27
  184.9 9.6 %reduce-scatter.7.cloned.1.call-done = f32[512,144]{1,0:T(8,128)} async-done(((f32[1024,144]{1,0:T(8,128)}), f32[512,144]{1,0:T(8,128)}) %reduce-scatter.7.cloned.1.call-update) | async-done | bytes 294928
  194.5 19.8 %reshape.266 = bf16[512,12,6,2]{3,2,1,0:T(8,128)(2,1)} reshape(f32[512,144]{1,0:T(8,128)} %reduce-scatter.7.cloned.1.call-done) | data formatting | bytes 442368
  214.3 12.8 %copy.64 = bf16[2,12,6,512]{3,0,2,1:T(2,128)(2,1)} copy(bf16[2,12,6,512]{0,2,1,3:T(8,128)(2,1)} %bitcast.72) | data formatting | bytes 294912
  227.1 695.5 %reduce-scatter.5.cloned.1.call-done = f32[8,1536]{1,0:T(8,128)} async-done(((f32[1024,1536]{1,0:T(8,128)}), f32[8,1536]{1,0:T(8,128)}) %reduce-scatter.5.cloned.1.call-update) | async-done | bytes 49168 | tf_op jit(solution)/shard_map/reduce_scatter | solution.py:144
  (50 shorter events, 14.2 us)
Async XLA Ops:
  7.2 55.4 %copy-start = (bf16[512,1024]{1,0:T(8,128)(2,1)S(1)}, bf16[512,1024]{1,0:T(8,128)(2,1)}, u32[]{:S(2)}) copy-start(bf16[512,1024]{1,0:T(8,128)(2,1)} %param.10) | copy-start | bytes 3145732
  7.2 187.3 %reduce-scatter.7.cloned.1.call-start = ((), (), s32[]{:S(2)}) async-start(), calls=%async_computation.3 | async-start | bytes 1572864
  11.0 20.5 %copy-start.4 = (s32[24]{0:T(128)S(1)}, s32[24]{0:T(128)}, u32[]{:S(2)}) copy-start(s32[24]{0:T(128)} %param.11) | copy-start | bytes 292
  11.0 15.4 %collective-permute-start = (bf16[2,2,12,6,1024]{4,1,3,2,0:T(2,128)(2,1)S(1)}, bf16[2,2,12,6,1024]{4,1,3,2,0:T(2,128)(2,1)S(1)}, u32[]{:S(2)}, u32[]{:S(2)}) collective-permute-start(bf16[2,2,12,6,1024]{4,1,3,2,0:T(2,128)(2,1)S(1)} %all_gather.3), channel_id=1, source_target_pairs={{4,0},{8,4},{12,8},{16,12},{20,16},{24,20},{28,24},{32,28},{36,32}... | collective-permute-start | bytes 1769480 | tf_op jit(solution)/shard_map/ppermute | solution.py:14
  26.8 28.8 %collective-permute-start.1 = (bf16[2,2,12,12,1024]{4,1,3,2,0:T(2,128)(2,1)S(1)}, bf16[2,2,12,12,1024]{4,1,3,2,0:T(2,128)(2,1)S(1)}, u32[]{:S(2)}, u32[]{:S(2)}) collective-permute-start(bf16[2,2,12,12,1024]{4,1,3,2,0:T(2,128)(2,1)S(1)} %constant_dynamic-update-slice_fusion), channel_id=1, source_target_pairs={{2,0},{0,2},{3,1},{1,3},{6,4},{4,6},{7,5},{5,7},{10,8},{8,10},{11,... | collective-permute-start | bytes 3538952 | tf_op jit(solution)/shard_map/ppermute | solution.py:14
  71.4 3.6 copy-start.2
  78.8 15.4 %collective-permute-start.2 = (bf16[2,12,12,1024]{3,0,2,1:T(2,128)(2,1)S(1)}, bf16[2,12,12,1024]{3,0,2,1:T(2,128)(2,1)S(1)}, u32[]{:S(2)}, u32[]{:S(2)}) collective-permute-start(bf16[2,12,12,1024]{3,0,2,1:T(2,128)(2,1)S(1)} %slice.84), channel_id=1, source_target_pairs={{2,0},{0,2},{3,1},{1,3},{6,4},{4,6},{7,5},{5,7},{10,8},{8,10},{11,... | collective-permute-start | bytes 1769480 | tf_op jit(solution)/shard_map/ppermute | solution.py:14
  94.9 16.7 %collective-permute-start.3 = (f32[2,12,6,1024]{3,0,2,1:T(2,128)S(1)}, f32[2,12,6,1024]{3,0,2,1:T(2,128)S(1)}, u32[]{:S(2)}, u32[]{:S(2)}) collective-permute-start(f32[2,12,6,1024]{3,0,2,1:T(2,128)S(1)} %slice.55), channel_id=1, source_target_pairs={{252,0},{0,4},{4,8},{8,12},{12,16},{16,20},{20,24},{24,28},{28,32}... | collective-permute-start | bytes 1769480 | tf_op jit(solution)/shard_map/ppermute | solution.py:14
  180.2 0.9 copy-start.3
  180.2 742.4 %reduce-scatter.5.cloned.1.call-start = ((), (), s32[]{:S(2)}) async-start(), calls=%async_computation.2 | async-start | bytes 6340608 | tf_op jit(solution)/shard_map/reduce_scatter | solution.py:144
  214.3 708.3 %copy-start.1 = (bf16[512,1024]{1,0:T(8,128)(2,1)S(1)}, bf16[512,1024]{1,0:T(8,128)(2,1)}, u32[]{:S(2)}) copy-start(bf16[512,1024]{1,0:T(8,128)(2,1)} %param.10) | copy-start | bytes 3145732
Sparse Core Ops, SparseCore 0:
  180.4 14.0 reduce-scatter.6
  197.7 724.8 reduce-scatter.4
where the time goes:
time: 931 us; the launch traced here: 929 us
  waiting for transfers between devices  768 us (82%)
  local copies, waits for them, and re-layouts  106 us (11%)
  matrix products  21.9 us (2%)
  between operations  15.6 us (2%)
  starting transfers between devices  10.7 us (1%)
    reduce_scatter x1, waiting for transfers between devices, shards(): lax.psum_scatter(jnp.einsum('td,tc->dc', flat_in, grad_cat, preferred_ele...  696 us
    unnamed x15, local copies, waits for them, and re-layouts  102 us
    ppermute x4, waiting for transfers between devices, from_behind(): return lax.ppermute(block, axis, route)  63 us
  transfers between devices with their start and end apart: 6, of which 6 were waited for; matrix products, arithmetic and copies ran while one was open for 4% of the time, Pallas kernels for 0%

commit v1 on v0

v1 whole, which is shorter than its diff:
```python
import functools

import jax
import jax.numpy as jnp
from jax import lax
from jax.experimental import pallas as pl
from jax.experimental.pallas import tpu as pltpu
from jax.sharding import PartitionSpec as P

MESH = pl.DeviceIdType.MESH
HEAD_DIM = 64
LEV = 2
WLAT = 12
WLON = 6
NX = 4
NZ = 8
TOK = LEV * WLAT * WLON
COL = LEV * WLAT
EDGE = 80
SLOTS = 80
HALF_ROWS = WLAT // 2
EXT = TOK + 2 * EDGE
F32 = jnp.float32
BF16 = jnp.bfloat16


def nn(a, b):
    return lax.dot_general(a, b, (((1,), (0,)), ((), ())), preferred_element_type=F32)


def nt(a, b):
    return lax.dot_general(a, b, (((1,), (1,)), ((), ())), preferred_element_type=F32)


def tn(a, b):
    return lax.dot_general(a, b, (((0,), (0,)), ((), ())), preferred_element_type=F32)


def iota(shape, axis):
    return lax.broadcasted_iota(jnp.int32, shape, axis)


def by24(t):
    return (t * 171) >> 12


def by12(t):
    return (t * 342) >> 12


def by6(t):
    return (t * 43) >> 8


def one_hot(cond):
    return jnp.where(cond, 1.0, 0.0).astype(BF16)


def kernel(
    sizes,
    band_ref,
    lat_ref,
    lon_ref,
    tok_ref,
    gout_ref,
    wqkv_hbm,
    wout_hbm,
    gtok_ref,
    gw_ref,
    wqkv,
    wout,
    ext,
    lat_send,
    lat_recv,
    xg,
    go,
    bias,
    qkv,
    ga,
    gall,
    gsend,
    grecv,
    gin,
    gin_recv,
    back_send,
    back_recv,
    side_send,
    side_recv,
    pfull,
    ysend,
    yrecv,
    rz,
    zsend,
    zrecv,
    rx,
    xrecv,
    w_sem,
    halo_send_sem,
    halo_recv_sem,
    lat_send_sem,
    lat_recv_sem,
    core_send_sem,
    core_recv_sem,
    xg_send_sem,
    xg_recv_sem,
    relay_send_sem,
    relay_recv_sem,
    g_send_sem,
    g_recv_sem,
    y_send_sem,
    y_recv_sem,
    z_send_sem,
    z_recv_sem,
    x_send_sem,
    x_recv_sem,
):
    n_lon, n_lat, width, half = sizes
    n_ylo = n_lon // (NX * NZ)
    n_y = n_lat * n_ylo
    cut = half // NX
    lon = lax.axis_index("lon")
    lat = lax.axis_index("lat")
    core = lax.axis_index("head")
    x = lon % NX
    z = (lon // NX) % NZ
    ylo = lon // (NX * NZ)
    y = lat * n_ylo + ylo

    right = ((lon + 1) % n_lon, lat, core)
    left = ((lon + n_lon - 1) % n_lon, lat, core)
    across = (lon, (lat + 1) % n_lat, core)
    sibling = (lon, lat, 1 - core)

    def x_peer(d):
        return (lon - x + (x + d) % NX, lat, core)

    def y_peer(d):
        other = (y + d) % n_y
        return (lon + (other % n_ylo - ylo) * (NX * NZ), other // n_ylo, core)

    def z_peer(d):
        return (lon + ((z + d) % NZ - z) * NX, lat, core)

    partners = [right, left, across, sibling]
    partners += [x_peer(d) for d in range(1, NX)]
    partners += [y_peer(d) for d in range(1, n_y)]
    partners += [z_peer(d) for d in range(1, NZ)]

    def remote(src, dst, send_sem, recv_sem, device):
        return pltpu.make_async_remote_copy(
            src_ref=src,
            dst_ref=dst,
            send_sem=send_sem,
            recv_sem=recv_sem,
            device_id=device,
            device_id_type=MESH,
        )

    barrier = pltpu.get_barrier_semaphore()
    for partner in partners:
        pl.semaphore_signal(barrier, inc=1, device_id=partner, device_id_type=MESH)

    load_qkv = pltpu.make_async_copy(wqkv_hbm, wqkv, w_sem.at[0])
    load_out = pltpu.make_async_copy(wout_hbm, wout, w_sem.at[1])
    load_qkv.start()
    load_out.start()

    row_shift = lat_ref[0]
    col_shift = lon_ref[0]
    row_swap = jnp.where(row_shift > HALF_ROWS, 1, 0)
    col_swap = jnp.where(col_shift > WLON // 2, 1, 0)
    f = row_shift - WLAT * row_swap
    e = col_shift - WLON * col_swap

    ext[0, EDGE : EDGE + TOK] = tok_ref[...]
    ext[1, EDGE : EDGE + TOK] = gout_ref[...]

    t = iota((TOK, EXT), 0)
    u = iota((TOK, EXT), 1)
    row = t - WLAT * by12(t) + f
    stays = (row >= 0) & (row < WLAT)
    keep_hot = one_hot(stays & (u == t + (EDGE + COL * e + f)))

    s = iota((SLOTS, EXT), 0)
    u = iota((SLOTS, EXT), 1)
    send_hot = one_hot(
        (u == s + HALF_ROWS * by6(s) + (EDGE + COL * e + HALF_ROWS * row_swap))
        & (s < TOK // 2)
    )

    t = iota((TOK, SLOTS), 0)
    s = iota((TOK, SLOTS), 1)
    group = by12(t)
    row = t - WLAT * group + f
    leaves = (row < 0) | (row >= WLAT)
    wrapped = jnp.where(row < 0, row + WLAT, row - WLAT)
    take_hot = one_hot(leaves & (s == HALF_ROWS * group + wrapped - HALF_ROWS * row_swap))

    k_at = iota((TOK, TOK), 0)
    q_at = iota((TOK, TOK), 1)
    first_row = WLAT * ((lat + row_swap) % n_lat) + row_shift
    k_row = k_at - WLAT * by12(k_at)
    q_row = q_at - WLAT * by12(q_at)
    n_rows = WLAT * n_lat
    counts = jnp.zeros((TOK, TOK), jnp.int32)
    for r in range(WLAT):
        raw = first_row + r
        counts = jnp.where(k_row == r, band_ref[jnp.where(raw >= n_rows, raw - n_rows, raw)], counts)
    n_cols = WLON * n_lon
    k_col = by24(k_at) + (WLON * lon + e)
    k_col = jnp.where(k_col < 0, k_col + n_cols, k_col)
    k_col = jnp.where(k_col >= n_cols, k_col - n_cols, k_col)
    same_side = (k_row + first_row >= n_rows) == (q_row + first_row >= n_rows)
    allowed = ((k_col < counts) | (k_at == q_at)) & same_side
    bias[...] = jnp.where(allowed, 0.0, -1e30)

    pl.semaphore_wait(barrier, len(partners))

    halo = []
    for a in range(2):
        to_left = remote(
            ext.at[a, EDGE : 2 * EDGE],
            ext.at[a, EDGE + TOK : EXT],
            halo_send_sem.at[a, 0],
            halo_recv_sem.at[a, 0],
            left,
        )
        to_right = remote(
            ext.at[a, TOK : TOK + EDGE],
            ext.at[a, 0:EDGE],
            halo_send_sem.at[a, 1],
            halo_recv_sem.at[a, 1],
            right,
        )
        to_left.start()
        to_right.start()
        halo.append((to_left, to_right))

    sends = []
    over_lat = []
    kept = []
    for a in range(2):
        for copy in halo[a]:
            copy.wait_recv()
        wide = ext[a]
        lat_send[a] = nn(send_hot, wide).astype(BF16)
        copy = remote(
            lat_send.at[a], lat_recv.at[a], lat_send_sem.at[a], lat_recv_sem.at[a], across
        )
        copy.start()
        over_lat.append(copy)
        kept.append(nn(keep_hot, wide))
    sends += [copy for pair in halo for copy in pair]
    sends += over_lat

    over_core = []
    over_x = []
    for a in range(2):
        over_lat[a].wait_recv()
        window = (kept[a] + nn(take_hot, lat_recv[a])).astype(BF16)
        if a == 0:
            xg[0, core] = window
            mine = xg.at[0, core]
        else:
            go[core] = window
            mine = go.at[core]
        copy = remote(mine, mine, core_send_sem.at[a], core_recv_sem.at[a], sibling)
        copy.start()
        over_core.append(copy)
        if a == 0:
            for d in range(1, NX):
                copy = remote(
                    xg.at[0, core],
                    xg.at[d, core],
                    xg_send_sem.at[d],
                    xg_recv_sem.at[d],
                    x_peer(d),
                )
                copy.start()
                over_x.append(copy)
    sends += over_core + over_x

    load_qkv.wait()
    over_core[0].wait_recv()
    for j in range(3):
        total = nn(xg[0, 0], wqkv[j, :half]) + nn(xg[0, 1], wqkv[j, half:])
        qkv[j] = total.astype(BF16)
    load_out.wait()
    over_core[1].wait_recv()
    ga[...] = (nt(go[0], wout[:, :half]) + nt(go[1], wout[:, half:])).astype(BF16)

    relays = []
    for d in range(1, NX):
        over_x[d - 1].wait_recv()
        copy = remote(
            xg.at[d, core],
            xg.at[d, core],
            relay_send_sem.at[d],
            relay_recv_sem.at[d],
            sibling,
        )
        copy.start()
        relays.append(copy)
    sends += relays

    scale = HEAD_DIM ** (-0.5)
    over_g = {}
    for n in range(NX):
        d = (n + 1) % NX
        part = pl.ds(pl.multiple_of(((x + d) % NX) * cut, cut), cut)
        q_part, k_part, v_part = (qkv[j, :, part] for j in range(3))
        g_part = ga[:, part]
        outs = [[], [], []]
        for head in range(cut // HEAD_DIM):
            at = slice(head * HEAD_DIM, (head + 1) * HEAD_DIM)
            q, k, v, g = q_part[:, at], k_part[:, at], v_part[:, at], g_part[:, at]
            scores = jnp.where(bias[...] == 0.0, nt(k, q) * scale, -1e30)
            raised = jnp.exp(scores - jnp.max(scores, 0, keepdims=True))
            probs = raised * (1.0 / jnp.sum(raised, 0, keepdims=True))
            grad_probs = nt(v, g)
            inner = jnp.sum(probs * grad_probs, 0, keepdims=True)
            grad_scores = (probs * (grad_probs - inner) * scale).astype(BF16)
            outs[0].append(tn(grad_scores, k).astype(BF16))
            outs[1].append(nn(grad_scores, q).astype(BF16))
            outs[2].append(nn(probs.astype(BF16), g).astype(BF16))
        for j in range(3):
            joined = jnp.concatenate(outs[j], 1)
            gall[j, :, part] = joined
            gsend[d, :, j * cut : (j + 1) * cut] = joined
        if d:
            copy = remote(
                gsend.at[d], grecv.at[d], g_send_sem.at[d], g_recv_sem.at[d], x_peer(d)
            )
            copy.start()
            over_g[d] = copy
    sends += list(over_g.values())

    def grad_in(which):
        rows = pl.ds(pl.multiple_of(which * half, half), half)
        return (
            nt(gall[0], wqkv[0, rows]) + nt(gall[1], wqkv[1, rows]) + nt(gall[2], wqkv[2, rows])
        )

    gin[0] = grad_in(1 - core)
    to_sibling = remote(gin.at[0], gin_recv, core_send_sem.at[2], core_recv_sem.at[2], sibling)
    to_sibling.start()
    gin[1] = grad_in(core)

    for copy in relays:
        copy.wait_recv()
    for d in range(1, NX):
        over_g[d].wait_recv()
    blocks = pfull.shape[0]
    own = pfull.shape[2]
    for side in range(2):
        total = tn(xg[0, side], gsend[0])
        for d in range(1, NX):
            total = total + tn(xg[d, side], grecv[d])
        pfull[side * (blocks // 2) : (side + 1) * (blocks // 2)] = total.reshape(
            blocks // 2, n_lat, own, 3 * cut
        )

    def y_rows(which):
        lo = which % n_ylo
        return pfull[pl.ds(lo * (NZ * NX), NZ * NX), which // n_ylo]

    over_y = []
    for d in range(1, n_y):
        ysend[d] = y_rows((y + d) % n_y).reshape(NZ * NX * own, 3 * cut).astype(BF16)
        copy = remote(
            ysend.at[d], yrecv.at[d], y_send_sem.at[d], y_recv_sem.at[d], y_peer(d)
        )
        copy.start()
        over_y.append(copy)
    sends += over_y

    to_sibling.wait_recv()
    window = (gin[1] + gin_recv[...]).astype(BF16)
    s = iota((SLOTS, TOK), 0)
    t = iota((SLOTS, TOK), 1)
    group = by12(t)
    row = t - WLAT * group + f
    leaves = (row < 0) | (row >= WLAT)
    wrapped = jnp.where(row < 0, row + WLAT, row - WLAT)
    give_hot = one_hot(leaves & (s == HALF_ROWS * group + wrapped - HALF_ROWS * row_swap))
    back_send[...] = nn(give_hot, window).astype(BF16)
    over_lat_back = remote(
        back_send, back_recv, lat_send_sem.at[2], lat_recv_sem.at[2], across
    )
    over_lat_back.start()
    b = iota((TOK, TOK), 0)
    t = iota((TOK, TOK), 1)
    row = b - WLAT * by12(b) - f
    stay_hot = one_hot((row >= 0) & (row < WLAT) & (t == b - f))
    kept = nn(stay_hot, window)
    b = iota((TOK, SLOTS), 0)
    s = iota((TOK, SLOTS), 1)
    group = by12(b)
    row = b - WLAT * group
    was = row - f
    came = (was < 0) | (was >= WLAT)
    back_hot = one_hot(came & (s == HALF_ROWS * group + row - HALF_ROWS * row_swap))
    over_lat_back.wait_recv()
    grid = (kept + nn(back_hot, back_recv[...])).astype(BF16)
    s = iota((EDGE, TOK), 0)
    t = iota((EDGE, TOK), 1)
    place = t + COL * e
    side_send[0] = nn(one_hot((place < 0) & (s == place + EDGE)), grid).astype(BF16)
    side_send[1] = nn(one_hot((place >= TOK) & (s == place - TOK)), grid).astype(BF16)
    side_left = remote(
        side_send.at[0], side_recv.at[0], halo_send_sem.at[2, 0], halo_recv_sem.at[2, 0], left
    )
    side_right = remote(
        side_send.at[1], side_recv.at[1], halo_send_sem.at[2, 1], halo_recv_sem.at[2, 1], right
    )
    side_left.start()
    side_right.start()
    sends += [to_sibling, over_lat_back, side_left, side_right]
    b = iota((TOK, TOK), 0)
    t = iota((TOK, TOK), 1)
    home = nn(one_hot(b == t + COL * e), grid)

    total = y_rows(y).reshape(NZ * NX * own, 3 * cut)
    for d in range(1, n_y):
        over_y[d - 1].wait_recv()
        total = total + yrecv[d].astype(F32)
    rz[...] = total.reshape(NZ, NX * own, 3 * cut)
    over_z = []
    for d in range(1, NZ):
        zsend[d] = rz[(z + d) % NZ].astype(BF16)
        copy = remote(
            zsend.at[d], zrecv.at[d], z_send_sem.at[d], z_recv_sem.at[d], z_peer(d)
        )
        copy.start()
        over_z.append(copy)
    sends += over_z

    side_left.wait_recv()
    side_right.wait_recv()
    b = iota((TOK, EDGE), 0)
    s = iota((TOK, EDGE), 1)
    from_right = nn(one_hot(b == s + (TOK - EDGE)), side_recv[0])
    from_left = nn(one_hot(b == s), side_recv[1])
    gtok_ref[...] = (home + from_right + from_left).astype(BF16)

    total = rz[z]
    for d in range(1, NZ):
        over_z[d - 1].wait_recv()
        total = total + zrecv[d].astype(F32)
    rx[...] = total.reshape(NX, own, 3 * cut)
    last = []
    for d in range(1, NX):
        copy = remote(
            rx.at[(x + d) % NX], xrecv.at[d], x_send_sem.at[d], x_recv_sem.at[d], x_peer(d)
        )
        copy.start()
        last.append(copy)
    for d in range(NX):
        if d:
            last[d - 1].wait_recv()
            piece = xrecv[d]
        else:
            piece = rx[x]
        part = pl.ds(pl.multiple_of(((x + NX - d) % NX) * cut, cut), cut)
        for j in range(3):
            gw_ref[j, :, part] = piece[:, j * cut : (j + 1) * cut]
    sends += last

    for copy in sends:
        copy.wait_send()


def solution(mesh):
    n_lon, n_lat = mesh.shape["lon"], mesh.shape["lat"]

    def flat(array):
        return array.transpose(2, 0, 1, 3).reshape(TOK, array.shape[-1])

    def shards(tokens, grad_out, w_qkv, w_out, band_count, lat_shift, lon_shift):
        half = tokens.shape[-1]
        width = w_qkv.shape[1]
        own = width // (n_lon * n_lat)
        n_y = n_lon // (NX * NZ) * n_lat
        cut = half // NX
        vmem = pl.BlockSpec(memory_space=pltpu.VMEM)
        smem = pl.BlockSpec(memory_space=pltpu.SMEM)
        hbm = pl.BlockSpec(memory_space=pl.ANY)
        dma = pltpu.SemaphoreType.DMA
        gtok, gw = pl.pallas_call(
            functools.partial(kernel, (n_lon, n_lat, width, half)),
            out_shape=(
                jax.ShapeDtypeStruct((TOK, half), BF16),
                jax.ShapeDtypeStruct((3, own, half), F32),
            ),
            in_specs=[smem, smem, smem, vmem, vmem, hbm, hbm],
            out_specs=(vmem, vmem),
            scratch_shapes=[
                pltpu.VMEM((3, width, half), BF16),
                pltpu.VMEM((half, width), BF16),
                pltpu.VMEM((2, EXT, half), BF16),
                pltpu.VMEM((2, SLOTS, half), BF16),
                pltpu.VMEM((2, SLOTS, half), BF16),
                pltpu.VMEM((NX, 2, TOK, half), BF16),
                pltpu.VMEM((2, TOK, half), BF16),
                pltpu.VMEM((TOK, TOK), F32),
                pltpu.VMEM((3, TOK, half), BF16),
                pltpu.VMEM((TOK, half), BF16),
                pltpu.VMEM((3, TOK, half), BF16),
                pltpu.VMEM((NX, TOK, 3 * cut), BF16),
                pltpu.VMEM((NX, TOK, 3 * cut), BF16),
                pltpu.VMEM((2, TOK, half), F32),
                pltpu.VMEM((TOK, half), F32),
                pltpu.VMEM((SLOTS, half), BF16),
                pltpu.VMEM((SLOTS, half), BF16),
                pltpu.VMEM((2, EDGE, half), BF16),
                pltpu.VMEM((2, EDGE, half), BF16),
                pltpu.VMEM((n_lon, n_lat, own, 3 * cut), F32),
                pltpu.VMEM((n_y, NZ * NX * own, 3 * cut), BF16),
                pltpu.VMEM((n_y, NZ * NX * own, 3 * cut), BF16),
                pltpu.VMEM((NZ, NX * own, 3 * cut), F32),
                pltpu.VMEM((NZ, NX * own, 3 * cut), BF16),
                pltpu.VMEM((NZ, NX * own, 3 * cut), BF16),
                pltpu.VMEM((NX, own, 3 * cut), F32),
                pltpu.VMEM((NX, own, 3 * cut), F32),
                dma((2,)),
                dma((3, 2)),
                dma((3, 2)),
                dma((3,)),
                dma((3,)),
                dma((3,)),
                dma((3,)),
                dma((NX,)),
                dma((NX,)),
                dma((NX,)),
                dma((NX,)),
                dma((NX,)),
                dma((NX,)),
                dma((n_y,)),
                dma((n_y,)),
                dma((NZ,)),
                dma((NZ,)),
                dma((NX,)),
                dma((NX,)),
            ],
            compiler_params=pltpu.CompilerParams(
                collective_id=0, has_side_effects=True, vmem_limit_bytes=48 * 2**20
            ),
        )(band_count, lat_shift, lon_shift, flat(tokens), flat(grad_out), w_qkv, w_out)
        gtok = gtok.reshape(WLON, LEV, WLAT, half).transpose(1, 2, 0, 3)
        return gtok, gw

    in_specs = (
        P(None, "lat", "lon", "head"),
        P(None, "lat", "lon", "head"),
        P(None, None, "head"),
        P("head", None),
        P(),
        P(),
        P(),
    )
    out_specs = (P(None, "lat", "lon", "head"), P(None, ("lon", "lat"), "head"))
    return jax.shard_map(shards, mesh=mesh, in_specs=in_specs, out_specs=out_specs, check_vma=False)
```

time: 931 us -> 63.9 us (0.07)
  the two profiles are of different devices: /device:TPU:128 before, /device:TPU:16 now
where the time goes in v1:
time: 63.9 us; the launch traced here: 63.7 us
  Pallas kernels  54.5 us (85%)
  local copies, waits for them, and re-layouts  7.19 us (11%)
  between operations  1.98 us (3%)
    pallas_call x1, Pallas kernels, shards(): pl.pallas_call(functools.partial(kernel, (n_lon, n_lat, width, half)), ou...  54.5 us
    unnamed x8, local copies, waits for them, and re-layouts  5.2 us
    transpose x2, local copies, waits for them, and re-layouts, flat(): return array.transpose(2, 0, 1, 3).reshape(TOK, array.shape[-1])  1.88 us

profile of v1, /device:TPU:16, one launch (start us, length us, event | category | flops | bytes accessed | tf_op | source)
XLA Modules:
  0.0 63.7 jit_solution(18206282340909673390)
XLA Ops:
  1.9 0.9 %copy.12 = bf16[6,2,12,512]{3,2,1,0:T(8,128)(2,1)S(1)} copy(bf16[6,2,12,512]{3,1,0,2:T(2,128)(2,1)} %bitcast.4) | data formatting | bytes 294912 | tf_op jit(solution)/shard_map/transpose | solution.py:477
  2.9 0.9 %copy.13 = bf16[6,2,12,512]{3,2,1,0:T(8,128)(2,1)S(1)} copy(bf16[6,2,12,512]{3,1,0,2:T(2,128)(2,1)} %bitcast.5) | data formatting | bytes 294912 | tf_op jit(solution)/shard_map/transpose | solution.py:477
  3.9 0.0 copy-start
  3.9 1.9 %copy-done = bf16[3,1024,512]{2,1,0:T(8,128)(2,1)S(1)} copy-done((bf16[3,1024,512]{2,1,0:T(8,128)(2,1)S(1)}, bf16[3,1024,512]{2,1,0:T(8,128)(2,1)}, u32[]{:S(2)}) %copy-start) | copy-done | bytes 3145752
  5.8 0.0 copy-start.1
  5.8 1.2 %copy-done.1 = bf16[512,1024]{1,0:T(8,128)(2,1)S(1)} copy-done((bf16[512,1024]{1,0:T(8,128)(2,1)S(1)}, bf16[512,1024]{1,0:T(8,128)(2,1)}, u32[]{:S(2)}) %copy-start.1) | copy-done | bytes 1048600
  7.0 0.0 copy-start.2
  7.0 0.7 %copy-done.2 = s32[24]{0:T(128)S(1)} copy-done((s32[24]{0:T(128)S(1)}, s32[24]{0:T(128)}, u32[]{:S(2)}) %copy-start.2) | copy-done | bytes 120
  7.7 54.5 %shard_map.86 = (bf16[144,512]{1,0:T(8,128)(2,1)S(1)}, f32[3,8,512]{2,1,0:T(8,128)S(1)}) custom-call(s32[24]{0:T(128)S(1)} %copy-done.2, s32[1]{0:T(128)S(6)} %copy.16.lat_ref, s32[1]{0:T(128)S(6)} %copy.17.lon_ref, bf16[144,512]{1,0:T(8,128)(2,1)S(1)} %reshape.13.tok_ref, bf16[144,512]{1,0:T(8,128)(2,1)S(1)} %reshape.14.gout_ref, ...), custom_call_target="tpu_custom_call" | custom-call | tf_op jit(solution)/shard_map/pallas_call | solution.py:489
  62.2 0.8 %copy.14 = bf16[2,12,6,512]{3,0,2,1:T(2,128)(2,1)} copy(bf16[2,12,6,512]{3,1,0,2:T(8,128)(2,1)S(1)} %bitcast.3) | data formatting | bytes 294912
  63.0 0.6 copy.18
  (3 shorter events, 0.1 us)
Async XLA Ops:
  3.9 1.9 %copy-start = (bf16[3,1024,512]{2,1,0:T(8,128)(2,1)S(1)}, bf16[3,1024,512]{2,1,0:T(8,128)(2,1)}, u32[]{:S(2)}) copy-start(bf16[3,1024,512]{2,1,0:T(8,128)(2,1)} %wqkv_hbm.1) | copy-start | bytes 9437188
  5.8 1.2 %copy-start.1 = (bf16[512,1024]{1,0:T(8,128)(2,1)S(1)}, bf16[512,1024]{1,0:T(8,128)(2,1)}, u32[]{:S(2)}) copy-start(bf16[512,1024]{1,0:T(8,128)(2,1)} %wout_hbm.1) | copy-start | bytes 3145732
  7.0 0.7 %copy-start.2 = (s32[24]{0:T(128)S(1)}, s32[24]{0:T(128)}, u32[]{:S(2)}) copy-start(s32[24]{0:T(128)} %band_ref.1) | copy-start | bytes 292

commit v2 on v1

v2 whole, which is shorter than its diff:
```python
import functools

import jax
import jax.numpy as jnp
from jax import lax
from jax.experimental import pallas as pl
from jax.experimental.pallas import tpu as pltpu
from jax.sharding import PartitionSpec as P

MESH = pl.DeviceIdType.MESH
HEAD_DIM = 64
LEV = 2
WLAT = 12
WLON = 6
NX = 4
NZ = 8
TOK = LEV * WLAT * WLON
ROW = LEV * WLON
HALF_ROWS = WLAT // 2
HALF_COLS = WLON // 2
F32 = jnp.float32
BF16 = jnp.bfloat16


def nn(a, b):
    return lax.dot_general(a, b, (((1,), (0,)), ((), ())), preferred_element_type=F32)


def nt(a, b):
    return lax.dot_general(a, b, (((1,), (1,)), ((), ())), preferred_element_type=F32)


def tn(a, b):
    return lax.dot_general(a, b, (((0,), (0,)), ((), ())), preferred_element_type=F32)


def iota(shape, axis):
    return lax.broadcasted_iota(jnp.int32, shape, axis)


def by12(t):
    return (t * 342) >> 12


def kernel(
    sizes,
    band_ref,
    lat_ref,
    lon_ref,
    tok_hbm,
    gout_hbm,
    wqkv_hbm,
    wout_hbm,
    gtok_ref,
    gw_ref,
    wqkv,
    wout,
    tok_wide,
    gout_wide,
    tok_rows,
    gout_rows,
    lat_send,
    xo,
    xg,
    go,
    bias,
    qkv,
    ga,
    gall,
    own_qk,
    own_v,
    qk_recv,
    v_recv,
    gin,
    gin_recv,
    back_own,
    back_rows,
    back_send,
    side_own,
    side_cols,
    side_send,
    pw,
    pn,
    wsend,
    wrecv,
    nsend,
    nrecv,
    rz,
    zsend,
    zrecv,
    rw,
    rn,
    fw,
    fn,
    load_sem,
    halo_send_sem,
    halo_recv_sem,
    lat_send_sem,
    lat_recv_sem,
    core_send_sem,
    core_recv_sem,
    xg_send_sem,
    xg_recv_sem,
    relay_send_sem,
    relay_recv_sem,
    g_send_sem,
    g_recv_sem,
    p_send_sem,
    p_recv_sem,
    z_send_sem,
    z_recv_sem,
    f_send_sem,
    f_recv_sem,
):
    n_lon, n_lat, width, half = sizes
    n_ylo = n_lon // (NX * NZ)
    n_y = n_lat * n_ylo
    assert n_y == NX
    cut = half // NX
    lon = lax.axis_index("lon")
    lat = lax.axis_index("lat")
    core = lax.axis_index("head")
    x = lon % NX
    z = (lon // NX) % NZ
    ylo = lon // (NX * NZ)
    y = lat * n_ylo + ylo

    right = ((lon + 1) % n_lon, lat, core)
    left = ((lon + n_lon - 1) % n_lon, lat, core)
    across = (lon, (lat + 1) % n_lat, core)
    sibling = (lon, lat, 1 - core)

    def x_peer(d):
        return (lon - x + (x + d) % NX, lat, core)

    def y_peer(d):
        other = (y + d) % n_y
        return (lon + (other % n_ylo - ylo) * (NX * NZ), other // n_ylo, core)

    def z_peer(d):
        return (lon + ((z + d) % NZ - z) * NX, lat, core)

    def either(for_first, for_second):
        return for_first + core * (for_second - for_first)

    def wide_peer(d):
        return tuple(either(a, b) for a, b in zip(x_peer(d)[:2], y_peer(d)[:2])) + (core,)

    def slim_peer(d):
        return tuple(either(a, b) for a, b in zip(y_peer(d)[:2], x_peer(d)[:2])) + (core,)

    wide_at = either(x, y)
    slim_at = either(y, x)

    def x_block(i):
        return i * n_lat

    def y_block(i):
        return (i % n_ylo) * (NZ * NX * n_lat) + i // n_ylo

    def wide_block(i):
        return either(x_block(i), y_block(i))

    def slim_block(i):
        return either(y_block(i), x_block(i))

    partners = [right, left, across, sibling]
    partners += [x_peer(d) for d in range(1, NX)]
    partners += [y_peer(d) for d in range(1, n_y)]
    partners += [z_peer(d) for d in range(1, NZ)]

    def remote(src, dst, send_sem, recv_sem, device):
        return pltpu.make_async_remote_copy(
            src_ref=src,
            dst_ref=dst,
            send_sem=send_sem,
            recv_sem=recv_sem,
            device_id=device,
            device_id_type=MESH,
        )

    barrier = pltpu.get_barrier_semaphore()
    for partner in partners:
        pl.semaphore_signal(barrier, inc=1, device_id=partner, device_id_type=MESH)

    inputs = (tok_hbm, gout_hbm)
    wides = (tok_wide, gout_wide)
    rows_of = (tok_rows, gout_rows)
    loads = []
    for a in range(2):
        middle = wides[a].at[:, HALF_COLS : HALF_COLS + WLON]
        loads.append(pltpu.make_async_copy(inputs[a], middle, load_sem.at[a]))
    loads.append(pltpu.make_async_copy(wqkv_hbm, wqkv, load_sem.at[2]))
    loads.append(pltpu.make_async_copy(wout_hbm, wout, load_sem.at[3]))
    for load in loads:
        load.start()

    row_shift = lat_ref[0]
    col_shift = lon_ref[0]
    row_swap = jnp.where(row_shift > HALF_ROWS, 1, 0)
    col_swap = jnp.where(col_shift > HALF_COLS, 1, 0)
    f = row_shift - WLAT * row_swap
    e = col_shift - WLON * col_swap

    k_at = iota((TOK, TOK), 0)
    q_at = iota((TOK, TOK), 1)
    first_row = WLAT * ((lat + row_swap) % n_lat) + row_shift
    k_row = by12(k_at)
    q_row = by12(q_at)
    n_rows = WLAT * n_lat
    counts = jnp.zeros((TOK, TOK), jnp.int32)
    for r in range(WLAT):
        raw = first_row + r
        counts = jnp.where(k_row == r, band_ref[jnp.where(raw >= n_rows, raw - n_rows, raw)], counts)
    n_cols = WLON * n_lon
    k_col = ((k_at - ROW * k_row) >> 1) + (WLON * lon + e)
    k_col = jnp.where(k_col < 0, k_col + n_cols, k_col)
    k_col = jnp.where(k_col >= n_cols, k_col - n_cols, k_col)
    same_side = (k_row + first_row >= n_rows) == (q_row + first_row >= n_rows)
    allowed = ((k_col < counts) | (k_at == q_at)) & same_side
    bias[...] = jnp.where(allowed, 0.0, -1e30)

    pl.semaphore_wait(barrier, len(partners))

    halo = []
    for a in range(2):
        to_left = remote(
            inputs[a].at[:, 0:HALF_COLS],
            wides[a].at[:, HALF_COLS + WLON : 2 * WLON],
            halo_send_sem.at[a, 0],
            halo_recv_sem.at[a, 0],
            left,
        )
        to_right = remote(
            inputs[a].at[:, HALF_COLS:WLON],
            wides[a].at[:, 0:HALF_COLS],
            halo_send_sem.at[a, 1],
            halo_recv_sem.at[a, 1],
            right,
        )
        to_left.start()
        to_right.start()
        halo.append((to_left, to_right))

    sends = [copy for pair in halo for copy in pair]
    over_lat = []
    for a in range(2):
        loads[a].wait()
        for copy in halo[a]:
            copy.wait_recv()
        columns = pl.ds(e + HALF_COLS, WLON)
        lat_send[a] = wides[a][pl.ds(HALF_ROWS * row_swap, HALF_ROWS), columns]
        copy = remote(
            lat_send.at[a],
            rows_of[a].at[WLAT : WLAT + HALF_ROWS],
            lat_send_sem.at[a],
            lat_recv_sem.at[a],
            across,
        )
        copy.start()
        over_lat.append(copy)
        rows_of[a][0:WLAT] = wides[a][:, columns]
    sends += over_lat

    over_core = []
    over_plane = {}
    for a in range(2):
        over_lat[a].wait_recv()
        picked = []
        for r in range(WLAT):
            q = f + r
            place = jnp.where(q < 0, q + (WLAT + HALF_ROWS), q)
            picked.append(rows_of[a][place])
        window = jnp.stack(picked).reshape(TOK, half)
        if a == 0:
            xo[core] = window
            mine = xo.at[core]
        else:
            go[core] = window
            mine = go.at[core]
        copy = remote(mine, mine, core_send_sem.at[a], core_recv_sem.at[a], sibling)
        copy.start()
        over_core.append(copy)
        if a == 0:
            for d in range(1, NX):
                for axis, peer in ((0, x_peer(d)), (1, y_peer(d))):
                    copy = remote(
                        xo.at[core],
                        xg.at[axis, d, core],
                        xg_send_sem.at[axis, d],
                        xg_recv_sem.at[axis, d],
                        peer,
                    )
                    copy.start()
                    over_plane[axis, d] = copy
    sends += over_core + list(over_plane.values())

    loads[2].wait()
    over_core[0].wait_recv()
    for j in range(3):
        total = nn(xo[0], wqkv[j, :half]) + nn(xo[1], wqkv[j, half:])
        qkv[j] = total.astype(BF16)
    loads[3].wait()
    over_core[1].wait_recv()
    ga[...] = (nt(go[0], wout[:, :half]) + nt(go[1], wout[:, half:])).astype(BF16)

    scale = HEAD_DIM ** (-0.5)
    over_qk = {}
    for n in range(NX):
        d = (n + 1) % NX
        pair = (wide_at + d) % NX
        part = pl.ds(pl.multiple_of(pair * cut, cut), cut)
        q_part, k_part, v_part = (qkv[j, :, part] for j in range(3))
        g_part = ga[:, part]
        outs = [[], [], []]
        for head in range(cut // HEAD_DIM):
            at = slice(head * HEAD_DIM, (head + 1) * HEAD_DIM)
            q, k, v, g = q_part[:, at], k_part[:, at], v_part[:, at], g_part[:, at]
            scores = jnp.where(bias[...] == 0.0, nt(k, q) * scale, -1e30)
            raised = jnp.exp(scores - jnp.max(scores, 0, keepdims=True))
            probs = raised * (1.0 / jnp.sum(raised, 0, keepdims=True))
            grad_probs = nt(v, g)
            inner = jnp.sum(probs * grad_probs, 0, keepdims=True)
            grad_scores = (probs * (grad_probs - inner) * scale).astype(BF16)
            outs[0].append(tn(grad_scores, k).astype(BF16))
            outs[1].append(nn(grad_scores, q).astype(BF16))
            outs[2].append(nn(probs.astype(BF16), g).astype(BF16))
        for j in range(3):
            joined = jnp.concatenate(outs[j], 1)
            gall[j, :, part] = joined
            if j < 2:
                own_qk[d, :, j * cut : (j + 1) * cut] = joined
            else:
                own_v[pair] = joined
        if d:
            copy = remote(
                own_qk.at[d], qk_recv.at[d], g_send_sem.at[0, d], g_recv_sem.at[0, d], wide_peer(d)
            )
            copy.start()
            over_qk[d] = copy
    over_v = {}
    for d in range(1, NX):
        copy = remote(
            own_v.at[(slim_at + d) % NX],
            v_recv.at[d],
            g_send_sem.at[1, d],
            g_recv_sem.at[1, d],
            slim_peer(d),
        )
        copy.start()
        over_v[d] = copy
    sends += list(over_qk.values()) + list(over_v.values())

    def grad_in(which):
        rows = pl.ds(pl.multiple_of(which * half, half), half)
        return (
            nt(gall[0], wqkv[0, rows]) + nt(gall[1], wqkv[1, rows]) + nt(gall[2], wqkv[2, rows])
        )

    gin[0] = grad_in(1 - core)
    to_sibling = remote(gin.at[0], gin_recv, core_send_sem.at[2], core_recv_sem.at[2], sibling)
    to_sibling.start()
    relays = {}
    for key, copy in over_plane.items():
        axis, d = key
        copy.wait_recv()
        mine = xg.at[axis, d, core]
        relay = remote(mine, mine, relay_send_sem.at[axis, d], relay_recv_sem.at[axis, d], sibling)
        relay.start()
        relays[key] = relay
    gin[1] = grad_in(core)

    to_sibling.wait_recv()
    window = (gin[1] + gin_recv[...]).astype(BF16).reshape(WLAT, WLON, LEV, half)
    back_own[...] = window
    back_rows[0:WLAT] = window
    for k in range(HALF_ROWS):
        from_row = k + jnp.where(f > 0, WLAT, -HALF_ROWS) - f
        back_send[k] = back_own[jnp.clip(from_row, 0, WLAT - 1)]
    over_lat_back = remote(
        back_send,
        back_rows.at[WLAT : WLAT + HALF_ROWS],
        lat_send_sem.at[2],
        lat_recv_sem.at[2],
        across,
    )
    over_lat_back.start()

    for copy in relays.values():
        copy.wait_recv()
    for d in range(1, NX):
        over_qk[d].wait_recv()
        over_v[d].wait_recv()
    blocks = pw.shape[0]
    own = pw.shape[1]
    for side in range(2):
        rows = slice(side * (blocks // 2), (side + 1) * (blocks // 2))
        total = tn(xo[side], own_qk[0])
        for d in range(1, NX):
            total = total + tn(xg[core, d, side], qk_recv[d])
        pw[rows] = total.reshape(blocks // 2, own, 2 * cut)
        total = tn(xo[side], own_v[slim_at])
        for d in range(1, NX):
            total = total + tn(xg[1 - core, d, side], v_recv[d])
        pn[rows] = total.reshape(blocks // 2, own, cut)

    def wide_rows(i):
        picked = [
            pw[slim_block(i) + k * (NX * n_lat) + wide_block(s)] for k in range(NZ) for s in range(NX)
        ]
        return jnp.concatenate(picked, 0)

    def slim_rows(i):
        picked = [
            pn[wide_block(i) + k * (NX * n_lat) + slim_block(s)] for k in range(NZ) for s in range(NX)
        ]
        return jnp.concatenate(picked, 0)

    over_p = []
    for d in range(1, NX):
        wsend[d] = wide_rows((slim_at + d) % NX).astype(BF16)
        to_wide = remote(
            wsend.at[d], wrecv.at[d], p_send_sem.at[0, d], p_recv_sem.at[0, d], slim_peer(d)
        )
        to_wide.start()
        nsend[d] = slim_rows((wide_at + d) % NX).astype(BF16)
        to_slim = remote(
            nsend.at[d], nrecv.at[d], p_send_sem.at[1, d], p_recv_sem.at[1, d], wide_peer(d)
        )
        to_slim.start()
        over_p.append((to_wide, to_slim))
    sends += [copy for pair in over_p for copy in pair]

    over_lat_back.wait_recv()
    for b in range(WLAT):
        was = b - f
        home = (was >= 0) & (was < WLAT)
        row = back_rows[jnp.where(home, was, b + WLAT - HALF_ROWS * row_swap)]
        side_own[b] = row
        side_cols[b, 0:WLON] = row
    for s in range(HALF_COLS):
        side_send[0, :, s] = side_own[:, jnp.clip(s - HALF_COLS - e, 0, WLON - 1)]
        side_send[1, :, s] = side_own[:, jnp.clip(s + WLON - e, 0, WLON - 1)]
    side_left = remote(
        side_send.at[0],
        side_cols.at[:, WLON + HALF_COLS : 2 * WLON],
        halo_send_sem.at[2, 0],
        halo_recv_sem.at[2, 0],
        left,
    )
    side_right = remote(
        side_send.at[1],
        side_cols.at[:, WLON : WLON + HALF_COLS],
        halo_send_sem.at[2, 1],
        halo_recv_sem.at[2, 1],
        right,
    )
    side_left.start()
    side_right.start()
    sends += [to_sibling, over_lat_back, side_left, side_right] + list(relays.values())

    total_w = wide_rows(slim_at)
    total_n = slim_rows(wide_at)
    for d in range(1, NX):
        over_p[d - 1][0].wait_recv()
        total_w = total_w + wrecv[d].astype(F32)
        over_p[d - 1][1].wait_recv()
        total_n = total_n + nrecv[d].astype(F32)
    rz[:, :, : 2 * cut] = total_w.reshape(NZ, NX * own, 2 * cut)
    rz[:, :, 2 * cut :] = total_n.reshape(NZ, NX * own, cut)
    over_z = []
    for d in range(1, NZ):
        zsend[d] = rz[(z + d) % NZ].astype(BF16)
        copy = remote(
            zsend.at[d], zrecv.at[d], z_send_sem.at[d], z_recv_sem.at[d], z_peer(d)
        )
        copy.start()
        over_z.append(copy)
    sends += over_z

    side_left.wait_recv()
    side_right.wait_recv()
    for q in range(WLON):
        c = q - e
        home = (c >= 0) & (c < WLON)
        gtok_ref[:, q] = side_cols[:, jnp.where(home, c, q + WLON)]

    total = rz[z]
    for d in range(1, NZ):
        over_z[d - 1].wait_recv()
        total = total + zrecv[d].astype(F32)
    rw[...] = total[:, : 2 * cut].reshape(NX, own, 2 * cut)
    rn[...] = total[:, 2 * cut :].reshape(NX, own, cut)
    last = []
    for d in range(1, NX):
        to_wide = remote(
            rw.at[(wide_at + d) % NX],
            fw.at[d],
            f_send_sem.at[0, d],
            f_recv_sem.at[0, d],
            wide_peer(d),
        )
        to_wide.start()
        to_slim = remote(
            rn.at[(slim_at + d) % NX],
            fn.at[d],
            f_send_sem.at[1, d],
            f_recv_sem.at[1, d],
            slim_peer(d),
        )
        to_slim.start()
        last.append((to_wide, to_slim))
    for d in range(NX):
        if d:
            last[d - 1][0].wait_recv()
            last[d - 1][1].wait_recv()
            qk, v = fw[d], fn[d]
        else:
            qk, v = rw[wide_at], rn[slim_at]
        part = pl.ds(pl.multiple_of(((wide_at + NX - d) % NX) * cut, cut), cut)
        gw_ref[0, :, part] = qk[:, :cut]
        gw_ref[1, :, part] = qk[:, cut:]
        part = pl.ds(pl.multiple_of(((slim_at + NX - d) % NX) * cut, cut), cut)
        gw_ref[2, :, part] = v
    sends += [copy for pair in last for copy in pair]

    for copy in sends:
        copy.wait_send()


def solution(mesh):
    n_lon, n_lat = mesh.shape["lon"], mesh.shape["lat"]

    def shards(tokens, grad_out, w_qkv, w_out, band_count, lat_shift, lon_shift):
        half = tokens.shape[-1]
        width = w_qkv.shape[1]
        own = width // (n_lon * n_lat)
        cut = half // NX
        rest = NZ * NX * own
        vmem = pl.BlockSpec(memory_space=pltpu.VMEM)
        smem = pl.BlockSpec(memory_space=pltpu.SMEM)
        hbm = pl.BlockSpec(memory_space=pltpu.HBM)
        dma = pltpu.SemaphoreType.DMA
        gtok, gw = pl.pallas_call(
            functools.partial(kernel, (n_lon, n_lat, width, half)),
            out_shape=(
                jax.ShapeDtypeStruct((WLAT, WLON, LEV, half), BF16),
                jax.ShapeDtypeStruct((3, own, half), F32),
            ),
            in_specs=[smem, smem, smem, hbm, hbm, hbm, hbm],
            out_specs=(vmem, vmem),
            scratch_shapes=[
                pltpu.VMEM((3, width, half), BF16),
                pltpu.VMEM((half, width), BF16),
                pltpu.VMEM((WLAT, 2 * WLON, LEV, half), BF16),
                pltpu.VMEM((WLAT, 2 * WLON, LEV, half), BF16),
                pltpu.VMEM((WLAT + HALF_ROWS, WLON, LEV, half), BF16),
                pltpu.VMEM((WLAT + HALF_ROWS, WLON, LEV, half), BF16),
                pltpu.VMEM((2, HALF_ROWS, WLON, LEV, half), BF16),
                pltpu.VMEM((2, TOK, half), BF16),
                pltpu.VMEM((2, NX, 2, TOK, half), BF16),
                pltpu.VMEM((2, TOK, half), BF16),
                pltpu.VMEM((TOK, TOK), F32),
                pltpu.VMEM((3, TOK, half), BF16),
                pltpu.VMEM((TOK, half), BF16),
                pltpu.VMEM((3, TOK, half), BF16),
                pltpu.VMEM((NX, TOK, 2 * cut), BF16),
                pltpu.VMEM((NX, TOK, cut), BF16),
                pltpu.VMEM((NX, TOK, 2 * cut), BF16),
                pltpu.VMEM((NX, TOK, cut), BF16),
                pltpu.VMEM((2, TOK, half), F32),
                pltpu.VMEM((TOK, half), F32),
                pltpu.VMEM((WLAT, WLON, LEV, half), BF16),
                pltpu.VMEM((WLAT + HALF_ROWS, WLON, LEV, half), BF16),
                pltpu.VMEM((HALF_ROWS, WLON, LEV, half), BF16),
                pltpu.VMEM((WLAT, WLON, LEV, half), BF16),
                pltpu.VMEM((WLAT, 2 * WLON, LEV, half), BF16),
                pltpu.VMEM((2, WLAT, HALF_COLS, LEV, half), BF16),
                pltpu.VMEM((n_lon * n_lat, own, 2 * cut), F32),
                pltpu.VMEM((n_lon * n_lat, own, cut), F32),
                pltpu.VMEM((NX, rest, 2 * cut), BF16),
                pltpu.VMEM((NX, rest, 2 * cut), BF16),
                pltpu.VMEM((NX, rest, cut), BF16),
                pltpu.VMEM((NX, rest, cut), BF16),
                pltpu.VMEM((NZ, NX * own, 3 * cut), F32),
                pltpu.VMEM((NZ, NX * own, 3 * cut), BF16),
                pltpu.VMEM((NZ, NX * own, 3 * cut), BF16),
                pltpu.VMEM((NX, own, 2 * cut), F32),
                pltpu.VMEM((NX, own, cut), F32),
                pltpu.VMEM((NX, own, 2 * cut), F32),
                pltpu.VMEM((NX, own, cut), F32),
                dma((4,)),
                dma((3, 2)),
                dma((3, 2)),
                dma((3,)),
                dma((3,)),
                dma((3,)),
                dma((3,)),
                dma((2, NX)),
                dma((2, NX)),
                dma((2, NX)),
                dma((2, NX)),
                dma((2, NX)),
                dma((2, NX)),
                dma((2, NX)),
                dma((2, NX)),
                dma((NZ,)),
                dma((NZ,)),
                dma((2, NX)),
                dma((2, NX)),
            ],
            compiler_params=pltpu.CompilerParams(
                collective_id=0, has_side_effects=True, vmem_limit_bytes=48 * 2**20
            ),
        )(
            band_count,
            lat_shift,
            lon_shift,
            tokens.transpose(1, 2, 0, 3),
            grad_out.transpose(1, 2, 0, 3),
            w_qkv,
            w_out,
        )
        return gtok.transpose(2, 0, 1, 3), gw

    in_specs = (
        P(None, "lat", "lon", "head"),
        P(None, "lat", "lon", "head"),
        P(None, None, "head"),
        P("head", None),
        P(),
        P(),
        P(),
    )
    out_specs = (P(None, "lat", "lon", "head"), P(None, ("lon", "lat"), "head"))
    return jax.shard_map(shards, mesh=mesh, in_specs=in_specs, out_specs=out_specs, check_vma=False)
```

time: 63.9 us -> 60.3 us (0.944)
  the two profiles are of different devices: /device:TPU:16 before, /device:TPU:1 now
where the time goes in v2:
time: 60.3 us; the launch traced here: 60.1 us
  Pallas kernels  51.3 us (85%)
  local copies, waits for them, and re-layouts  6.86 us (11%)
  between operations  1.94 us (3%)
    pallas_call x1, Pallas kernels, shards(): pl.pallas_call(functools.partial(kernel, (n_lon, n_lat, width, half)), ou...  51.3 us
    unnamed x12, local copies, waits for them, and re-layouts  6.86 us

profile of v2, /device:TPU:1, one launch (start us, length us, event | category | flops | bytes accessed | tf_op | source)
XLA Modules:
  0.0 60.1 jit_solution(5297853493024549594)
XLA Ops:
  1.9 0.0 copy-start
  1.9 1.9 %copy-done = bf16[3,1024,512]{2,1,0:T(8,128)(2,1)S(1)} copy-done((bf16[3,1024,512]{2,1,0:T(8,128)(2,1)S(1)}, bf16[3,1024,512]{2,1,0:T(8,128)(2,1)}, u32[]{:S(2)}) %copy-start) | copy-done | bytes 3145752
  3.8 0.0 copy-start.1
  3.8 1.2 %copy-done.1 = bf16[512,1024]{1,0:T(8,128)(2,1)S(1)} copy-done((bf16[512,1024]{1,0:T(8,128)(2,1)S(1)}, bf16[512,1024]{1,0:T(8,128)(2,1)}, u32[]{:S(2)}) %copy-start.1) | copy-done | bytes 1048600
  5.0 0.0 copy-start.2
  5.0 0.9 %copy-done.2 = bf16[2,12,6,512]{3,0,2,1:T(2,128)(2,1)S(1)} copy-done((bf16[2,12,6,512]{3,0,2,1:T(2,128)(2,1)S(1)}, bf16[2,12,6,512]{3,0,2,1:T(2,128)(2,1)}, u32[]{:S(2)}) %copy-start.2) | copy-done | bytes 147480
  5.9 0.0 copy-start.3
  6.0 0.9 %copy-done.3 = bf16[2,12,6,512]{3,0,2,1:T(2,128)(2,1)S(1)} copy-done((bf16[2,12,6,512]{3,0,2,1:T(2,128)(2,1)S(1)}, bf16[2,12,6,512]{3,0,2,1:T(2,128)(2,1)}, u32[]{:S(2)}) %copy-start.3) | copy-done | bytes 147480
  6.9 0.0 copy-start.4
  6.9 0.7 %copy-done.4 = s32[24]{0:T(128)S(1)} copy-done((s32[24]{0:T(128)S(1)}, s32[24]{0:T(128)}, u32[]{:S(2)}) %copy-start.4) | copy-done | bytes 120
  7.5 51.3 %shard_map.86 = (bf16[12,6,2,512]{3,2,1,0:T(2,128)(2,1)S(1)}, f32[3,8,512]{2,1,0:T(8,128)S(1)}) custom-call(s32[24]{0:T(128)S(1)} %copy-done.4, s32[1]{0:T(128)S(6)} %copy.11.lat_ref, s32[1]{0:T(128)S(6)} %copy.12.lon_ref, bf16[12,6,2,512]{3,2,1,0:T(2,128)(2,1)S(1)} %bitcast.4, bf16[12,6,2,512]{3,2,1,0:T(2,128)(2,1)S(1)} %bitcast.5, ...), custom_call_target="tpu_custom_call" | custom-call | tf_op jit(solution)/shard_map/pallas_call | solution.py:544
  58.8 0.7 %copy.13 = bf16[2,12,6,512]{3,0,2,1:T(2,128)(2,1)} copy(bf16[2,12,6,512]{3,0,2,1:T(2,128)(2,1)S(1)} %bitcast.3) | data formatting | bytes 294912
  59.5 0.6 %copy.14 = f32[3,8,512]{2,1,0:T(8,128)} copy(f32[3,8,512]{2,1,0:T(8,128)S(1)} %get-tuple-element.9) | data formatting | bytes 98304
Async XLA Ops:
  1.9 1.9 %copy-start = (bf16[3,1024,512]{2,1,0:T(8,128)(2,1)S(1)}, bf16[3,1024,512]{2,1,0:T(8,128)(2,1)}, u32[]{:S(2)}) copy-start(bf16[3,1024,512]{2,1,0:T(8,128)(2,1)} %wqkv_hbm.1) | copy-start | bytes 9437188
  3.8 1.2 %copy-start.1 = (bf16[512,1024]{1,0:T(8,128)(2,1)S(1)}, bf16[512,1024]{1,0:T(8,128)(2,1)}, u32[]{:S(2)}) copy-start(bf16[512,1024]{1,0:T(8,128)(2,1)} %wout_hbm.1) | copy-start | bytes 3145732
  5.0 0.9 %copy-start.2 = (bf16[2,12,6,512]{3,0,2,1:T(2,128)(2,1)S(1)}, bf16[2,12,6,512]{3,0,2,1:T(2,128)(2,1)}, u32[]{:S(2)}) copy-start(bf16[2,12,6,512]{3,0,2,1:T(2,128)(2,1)} %param.7) | copy-start | bytes 442372
  5.9 0.9 %copy-start.3 = (bf16[2,12,6,512]{3,0,2,1:T(2,128)(2,1)S(1)}, bf16[2,12,6,512]{3,0,2,1:T(2,128)(2,1)}, u32[]{:S(2)}) copy-start(bf16[2,12,6,512]{3,0,2,1:T(2,128)(2,1)} %param.8) | copy-start | bytes 442372
  6.9 0.7 %copy-start.4 = (s32[24]{0:T(128)S(1)}, s32[24]{0:T(128)}, u32[]{:S(2)}) copy-start(s32[24]{0:T(128)} %band_ref.1) | copy-start | bytes 292

commit v3 on v2

--- a/solution.py
+++ b/solution.py
@@ -68,9 +68,7 @@
     ga,
     gall,
     own_qk,
-    own_v,
-    qk_recv,
-    v_recv,
+    g_recv,
     gin,
     gin_recv,
     back_own,
@@ -79,19 +77,14 @@
     side_own,
     side_cols,
     side_send,
-    pw,
-    pn,
-    wsend,
-    wrecv,
-    nsend,
-    nrecv,
+    parts,
+    psend,
+    precv,
     rz,
     zsend,
     zrecv,
-    rw,
-    rn,
-    fw,
-    fn,
+    rf,
+    frecv,
     load_sem,
     halo_send_sem,
     halo_recv_sem,
@@ -304,58 +297,63 @@
     over_core[1].wait_recv()
     ga[...] = (nt(go[0], wout[:, :half]) + nt(go[1], wout[:, half:])).astype(BF16)
 
+    def factor_peer(t, d):
+        return wide_peer(d) if t < 2 else slim_peer(d)
+
+    def sum_peer(t, d):
+        return slim_peer(d) if t < 2 else wide_peer(d)
+
     scale = HEAD_DIM ** (-0.5)
-    over_qk = {}
-    for n in range(NX):
-        d = (n + 1) % NX
-        pair = (wide_at + d) % NX
-        part = pl.ds(pl.multiple_of(pair * cut, cut), cut)
-        q_part, k_part, v_part = (qkv[j, :, part] for j in range(3))
-        g_part = ga[:, part]
-        outs = [[], [], []]
-        for head in range(cut // HEAD_DIM):
-            at = slice(head * HEAD_DIM, (head + 1) * HEAD_DIM)
-            q, k, v, g = q_part[:, at], k_part[:, at], v_part[:, at], g_part[:, at]
+    over_g = {}
+    for t in range(2):
+        at = slice(t * HEAD_DIM, (t + 1) * HEAD_DIM)
+        for n in range(NX):
+            d = (n + 1) % NX
+            pair = (wide_at + d) % NX
+            lanes = pl.ds(pl.multiple_of(pair * cut, cut), cut)
+            q, k, v = (qkv[j, :, lanes][:, at] for j in range(3))
+            g = ga[:, lanes][:, at]
             scores = jnp.where(bias[...] == 0.0, nt(k, q) * scale, -1e30)
             raised = jnp.exp(scores - jnp.max(scores, 0, keepdims=True))
             probs = raised * (1.0 / jnp.sum(raised, 0, keepdims=True))
             grad_probs = nt(v, g)
             inner = jnp.sum(probs * grad_probs, 0, keepdims=True)
             grad_scores = (probs * (grad_probs - inner) * scale).astype(BF16)
-            outs[0].append(tn(grad_scores, k).astype(BF16))
-            outs[1].append(nn(grad_scores, q).astype(BF16))
-            outs[2].append(nn(probs.astype(BF16), g).astype(BF16))
-        for j in range(3):
-            joined = jnp.concatenate(outs[j], 1)
-            gall[j, :, part] = joined
-            if j < 2:
-                own_qk[d, :, j * cut : (j + 1) * cut] = joined
-            else:
-                own_v[pair] = joined
-        if d:
-            copy = remote(
-                own_qk.at[d], qk_recv.at[d], g_send_sem.at[0, d], g_recv_sem.at[0, d], wide_peer(d)
-            )
-            copy.start()
-            over_qk[d] = copy
-    over_v = {}
+            grad_q = tn(grad_scores, k).astype(BF16)
+            grad_k = nn(grad_scores, q).astype(BF16)
+            gall[0, pair, :, at] = grad_q
+            gall[1, pair, :, at] = grad_k
+            gall[2, pair, :, at] = nn(probs.astype(BF16), g).astype(BF16)
+            own_qk[t, d] = jnp.concatenate([grad_q, grad_k], 1)
+            if d:
+                copy = remote(
+                    own_qk.at[t, d],
+                    g_recv.at[t, d],
+                    g_send_sem.at[t, d],
+                    g_recv_sem.at[t, d],
+                    factor_peer(t, d),
+                )
+                copy.start()
+                over_g[t, d] = copy
     for d in range(1, NX):
         copy = remote(
-            own_v.at[(slim_at + d) % NX],
-            v_recv.at[d],
-            g_send_sem.at[1, d],
-            g_recv_sem.at[1, d],
-            slim_peer(d),
+            gall.at[2, (slim_at + d) % NX],
+            g_recv.at[2, d],
+            g_send_sem.at[2, d],
+            g_recv_sem.at[2, d],
+            factor_peer(2, d),
         )
         copy.start()
-        over_v[d] = copy
-    sends += list(over_qk.values()) + list(over_v.values())
+        over_g[2, d] = copy
+    sends += list(over_g.values())
 
     def grad_in(which):
         rows = pl.ds(pl.multiple_of(which * half, half), half)
-        return (
-            nt(gall[0], wqkv[0, rows]) + nt(gall[1], wqkv[1, rows]) + nt(gall[2], wqkv[2, rows])
-        )
+        total = 0.0
+        for j in range(3):
+            joined = jnp.concatenate([gall[j, pair] for pair in range(NX)], 1)
+            total = total + nt(joined, wqkv[j, rows])
+        return total
 
     gin[0] = grad_in(1 - core)
     to_sibling = remote(gin.at[0], gin_recv, core_send_sem.at[2], core_recv_sem.at[2], sibling)
@@ -386,50 +384,50 @@
     )
     over_lat_back.start()
 
-    for copy in relays.values():
-        copy.wait_recv()
-    for d in range(1, NX):
-        over_qk[d].wait_recv()
-        over_v[d].wait_recv()
-    blocks = pw.shape[0]
-    own = pw.shape[1]
-    for side in range(2):
-        rows = slice(side * (blocks // 2), (side + 1) * (blocks // 2))
-        total = tn(xo[side], own_qk[0])
+    blocks = parts.shape[1]
+    own = parts.shape[2]
+
+    def make_product(t):
+        axis = core if t < 2 else 1 - core
+        halves = []
+        for side in range(2):
+            halves.append(tn(xo[side], own_qk[t, 0] if t < 2 else gall[2, slim_at]))
         for d in range(1, NX):
-            total = total + tn(xg[core, d, side], qk_recv[d])
-        pw[rows] = total.reshape(blocks // 2, own, 2 * cut)
-        total = tn(xo[side], own_v[slim_at])
+            if t == 0:
+                relays[0, d].wait_recv()
+                relays[1, d].wait_recv()
+            over_g[t, d].wait_recv()
+            for side in range(2):
+                halves[side] = halves[side] + tn(xg[axis, d, side], g_recv[t, d])
+        for side in range(2):
+            rows = slice(side * (blocks // 2), (side + 1) * (blocks // 2))
+            parts[t, rows] = halves[side].reshape(blocks // 2, own, cut)
+
+    def owner_rows(t, i):
+        base = slim_block(i) if t < 2 else wide_block(i)
+        picked = []
+        for k in range(NZ):
+            for j in range(NX):
+                along = wide_block(j) if t < 2 else slim_block(j)
+                picked.append(parts[t, base + along + k * (NX * n_lat)])
+        return jnp.concatenate(picked, 0)
+
+    over_p = {}
+    for t in range(3):
+        make_product(t)
+        place = slim_at if t < 2 else wide_at
         for d in range(1, NX):
-            total = total + tn(xg[1 - core, d, side], v_recv[d])
-        pn[rows] = total.reshape(blocks // 2, own, cut)
-
-    def wide_rows(i):
-        picked = [
-            pw[slim_block(i) + k * (NX * n_lat) + wide_block(s)] for k in range(NZ) for s in range(NX)
-        ]
-        return jnp.concatenate(picked, 0)
-
-    def slim_rows(i):
-        picked = [
-            pn[wide_block(i) + k * (NX * n_lat) + slim_block(s)] for k in range(NZ) for s in range(NX)
-        ]
-        return jnp.concatenate(picked, 0)
-
-    over_p = []
-    for d in range(1, NX):
-        wsend[d] = wide_rows((slim_at + d) % NX).astype(BF16)
-        to_wide = remote(
-            wsend.at[d], wrecv.at[d], p_send_sem.at[0, d], p_recv_sem.at[0, d], slim_peer(d)
-        )
-        to_wide.start()
-        nsend[d] = slim_rows((wide_at + d) % NX).astype(BF16)
-        to_slim = remote(
-            nsend.at[d], nrecv.at[d], p_send_sem.at[1, d], p_recv_sem.at[1, d], wide_peer(d)
-        )
-        to_slim.start()
-        over_p.append((to_wide, to_slim))
-    sends += [copy for pair in over_p for copy in pair]
+            psend[t, d] = owner_rows(t, (place + d) % NX).astype(BF16)
+            copy = remote(
+                psend.at[t, d],
+                precv.at[t, d],
+                p_send_sem.at[t, d],
+                p_recv_sem.at[t, d],
+                sum_peer(t, d),
+            )
+            copy.start()
+            over_p[t, d] = copy
+    sends += list(over_p.values())
 
     over_lat_back.wait_recv()
     for b in range(WLAT):
@@ -459,24 +457,25 @@
     side_right.start()
     sends += [to_sibling, over_lat_back, side_left, side_right] + list(relays.values())
 
-    total_w = wide_rows(slim_at)
-    total_n = slim_rows(wide_at)
-    for d in range(1, NX):
-        over_p[d - 1][0].wait_recv()
-        total_w = total_w + wrecv[d].astype(F32)
-        over_p[d - 1][1].wait_recv()
-        total_n = total_n + nrecv[d].astype(F32)
-    rz[:, :, : 2 * cut] = total_w.reshape(NZ, NX * own, 2 * cut)
-    rz[:, :, 2 * cut :] = total_n.reshape(NZ, NX * own, cut)
-    over_z = []
-    for d in range(1, NZ):
-        zsend[d] = rz[(z + d) % NZ].astype(BF16)
-        copy = remote(
-            zsend.at[d], zrecv.at[d], z_send_sem.at[d], z_recv_sem.at[d], z_peer(d)
-        )
-        copy.start()
-        over_z.append(copy)
-    sends += over_z
+    over_z = {}
+    for t in range(3):
+        total = owner_rows(t, slim_at if t < 2 else wide_at)
+        for d in range(1, NX):
+            over_p[t, d].wait_recv()
+            total = total + precv[t, d].astype(F32)
+        rz[t] = total.reshape(NZ, NX * own, cut)
+        for d in range(1, NZ):
+            zsend[t, d] = rz[t, (z + d) % NZ].astype(BF16)
+            copy = remote(
+                zsend.at[t, d],
+                zrecv.at[t, d],
+                z_send_sem.at[t, d],
+                z_recv_sem.at[t, d],
+                z_peer(d),
+            )
+            copy.start()
+            over_z[t, d] = copy
+    sends += list(over_z.values())
 
     side_left.wait_recv()
     side_right.wait_recv()
@@ -485,44 +484,41 @@
         home = (c >= 0) & (c < WLON)
         gtok_ref[:, q] = side_cols[:, jnp.where(home, c, q + WLON)]
 
-    total = rz[z]
-    for d in range(1, NZ):
-        over_z[d - 1].wait_recv()
-        total = total + zrecv[d].astype(F32)
-    rw[...] = total[:, : 2 * cut].reshape(NX, own, 2 * cut)
-    rn[...] = total[:, 2 * cut :].reshape(NX, own, cut)
-    last = []
-    for d in range(1, NX):
-        to_wide = remote(
-            rw.at[(wide_at + d) % NX],
-            fw.at[d],
-            f_send_sem.at[0, d],
-            f_recv_sem.at[0, d],
-            wide_peer(d),
-        )
-        to_wide.start()
-        to_slim = remote(
-            rn.at[(slim_at + d) % NX],
-            fn.at[d],
-            f_send_sem.at[1, d],
-            f_recv_sem.at[1, d],
-            slim_peer(d),
-        )
-        to_slim.start()
-        last.append((to_wide, to_slim))
+    last = {}
+    for t in range(3):
+        total = rz[t, z]
+        for d in range(1, NZ):
+            over_z[t, d].wait_recv()
+            total = total + zrecv[t, d].astype(F32)
+        rf[:, t] = total.reshape(NX, own, cut)
+        if t == 0:
+            continue
+        group = slice(0, 2) if t == 1 else slice(2, 3)
+        place = wide_at if t == 1 else slim_at
+        for d in range(1, NX):
+            copy = remote(
+                rf.at[(place + d) % NX, group],
+                frecv.at[d, group],
+                f_send_sem.at[t, d],
+                f_recv_sem.at[t, d],
+                factor_peer(t, d),
+            )
+            copy.start()
+            last[t, d] = copy
+    sends += list(last.values())
     for d in range(NX):
         if d:
-            last[d - 1][0].wait_recv()
-            last[d - 1][1].wait_recv()
-            qk, v = fw[d], fn[d]
+            last[1, d].wait_recv()
+            last[2, d].wait_recv()
+            first, second, values = (frecv[d, t] for t in range(3))
         else:
-            qk, v = rw[wide_at], rn[slim_at]
-        part = pl.ds(pl.multiple_of(((wide_at + NX - d) % NX) * cut, cut), cut)
-        gw_ref[0, :, part] = qk[:, :cut]
-        gw_ref[1, :, part] = qk[:, cut:]
-        part = pl.ds(pl.multiple_of(((slim_at + NX - d) % NX) * cut, cut), cut)
-        gw_ref[2, :, part] = v
-    sends += [copy for pair in last for copy in pair]
+            first, second, values = rf[wide_at, 0], rf[wide_at, 1], rf[slim_at, 2]
+        lanes = pl.ds(pl.multiple_of(((wide_at + NX - d) % NX) * cut, cut), cut)
+        for j in range(2):
+            at = slice(j * HEAD_DIM, (j + 1) * HEAD_DIM)
+            gw_ref[j, :, lanes] = jnp.concatenate([first[:, at], second[:, at]], 1)
+        lanes = pl.ds(pl.multiple_of(((slim_at + NX - d) % NX) * cut, cut), cut)
+        gw_ref[2, :, lanes] = values
 
     for copy in sends:
         copy.wait_send()
@@ -563,11 +559,9 @@
                 pltpu.VMEM((TOK, TOK), F32),
                 pltpu.VMEM((3, TOK, half), BF16),
                 pltpu.VMEM((TOK, half), BF16),
-                pltpu.VMEM((3, TOK, half), BF16),
-                pltpu.VMEM((NX, TOK, 2 * cut), BF16),
-                pltpu.VMEM((NX, TOK, cut), BF16),
-                pltpu.VMEM((NX, TOK, 2 * cut), BF16),
-                pltpu.VMEM((NX, TOK, cut), BF16),
+                pltpu.VMEM((3, NX, TOK, cut), BF16),
+                pltpu.VMEM((2, NX, TOK, cut), BF16),
+                pltpu.VMEM((3, NX, TOK, cut), BF16),
                 pltpu.VMEM((2, TOK, half), F32),
                 pltpu.VMEM((TOK, half), F32),
                 pltpu.VMEM((WLAT, WLON, LEV, half), BF16),
@@ -576,19 +570,14 @@
                 pltpu.VMEM((WLAT, WLON, LEV, half), BF16),
                 pltpu.VMEM((WLAT, 2 * WLON, LEV, half), BF16),
                 pltpu.VMEM((2, WLAT, HALF_COLS, LEV, half), BF16),
-                pltpu.VMEM((n_lon * n_lat, own, 2 * cut), F32),
-                pltpu.VMEM((n_lon * n_lat, own, cut), F32),
-                pltpu.VMEM((NX, rest, 2 * cut), BF16),
-                pltpu.VMEM((NX, rest, 2 * cut), BF16),
-                pltpu.VMEM((NX, rest, cut), BF16),
-                pltpu.VMEM((NX, rest, cut), BF16),
-                pltpu.VMEM((NZ, NX * own, 3 * cut), F32),
-                pltpu.VMEM((NZ, NX * own, 3 * cut), BF16),
-                pltpu.VMEM((NZ, NX * own, 3 * cut), BF16),
-                pltpu.VMEM((NX, own, 2 * cut), F32),
-                pltpu.VMEM((NX, own, cut), F32),
-                pltpu.VMEM((NX, own, 2 * cut), F32),
-                pltpu.VMEM((NX, own, cut), F32),
+                pltpu.VMEM((3, n_lon * n_lat, own, cut), F32),
+                pltpu.VMEM((3, NX, rest, cut), BF16),
+                pltpu.VMEM((3, NX, rest, cut), BF16),
+                pltpu.VMEM((3, NZ, NX * own, cut), F32),
+                pltpu.VMEM((3, NZ, NX * own, cut), BF16),
+                pltpu.VMEM((3, NZ, NX * own, cut), BF16),
+                pltpu.VMEM((NX, 3, own, cut), F32),
+                pltpu.VMEM((NX, 3, own, cut), F32),
                 dma((4,)),
                 dma((3, 2)),
                 dma((3, 2)),
@@ -600,17 +589,17 @@
                 dma((2, NX)),
                 dma((2, NX)),
                 dma((2, NX)),
-                dma((2, NX)),
-                dma((2, NX)),
-                dma((2, NX)),
-                dma((2, NX)),
-                dma((NZ,)),
-                dma((NZ,)),
-                dma((2, NX)),
-                dma((2, NX)),
+                dma((3, NX)),
+                dma((3, NX)),
+                dma((3, NX)),
+                dma((3, NX)),
+                dma((3, NZ)),
+                dma((3, NZ)),
+                dma((3, NX)),
+                dma((3, NX)),
             ],
             compiler_params=pltpu.CompilerParams(
-                collective_id=0, has_side_effects=True, vmem_limit_bytes=48 * 2**20
+                collective_id=0, has_side_effects=True, vmem_limit_bytes=60 * 2**20
             ),
         )(
             band_count,

time: 60.3 us -> 55.9 us (0.927)
  local copies, waits for them, and re-layouts: 6.86 us -> 3.09 us
  Pallas kernels: 51.3 us -> 50.6 us
    unnamed x12 -> x2, local copies, waits for them, and re-layouts: 6.86 us -> 3.09 us
    pallas_call x1, Pallas kernels: 51.3 us -> 50.6 us  [shards(): pl.pallas_call(functools.partial(kernel, (n_lon, n_lat, width, half)), ou...]
where the time goes in v3:
time: 55.9 us; the launch traced here: 55.7 us
  Pallas kernels  50.6 us (91%)
  local copies, waits for them, and re-layouts  3.09 us (6%)
  between operations  1.93 us (3%)
    pallas_call x1, Pallas kernels, shards(): pl.pallas_call(functools.partial(kernel, (n_lon, n_lat, width, half)), ou...  50.6 us
    unnamed x2, local copies, waits for them, and re-layouts  3.09 us

profile of v3, /device:TPU:1, one launch (start us, length us, event | category | flops | bytes accessed | tf_op | source)
XLA Modules:
  0.0 55.7 jit_solution(16669343789791824534)
XLA Ops:
  1.9 50.6 %shard_map.86 = (bf16[12,6,2,512]{3,2,1,0:T(2,128)(2,1)}, f32[3,8,512]{2,1,0:T(8,128)}) custom-call(s32[24]{0:T(128)} %band_ref.1, s32[1]{0:T(128)S(6)} %copy.11.lat_ref, s32[1]{0:T(128)S(6)} %copy.12.lon_ref, bf16[12,6,2,512]{3,2,1,0:T(2,128)(2,1)} %bitcast.4, bf16[12,6,2,512]{3,2,1,0:T(2,128)(2,1)} %bitcast.5, bf16[3,1024,512]{2,1,0:T(8,128)(2,1)} %wqkv_hbm.1, ...), custom_call_target="tpu_custom_call" | custom-call | tf_op jit(solution)/shard_map/pallas_call | solution.py:540
  52.6 1.7 %copy.13 = bf16[2,12,6,512]{3,0,2,1:T(2,128)(2,1)} copy(bf16[2,12,6,512]{3,0,2,1:T(2,128)(2,1)} %bitcast.3) | data formatting | bytes 294912
  54.2 1.4 %copy.14 = f32[3,8,512]{2,1,0:T(8,128)} copy(f32[3,8,512]{2,1,0:T(8,128)} %get-tuple-element.9) | data formatting | bytes 98304

commit v4 on v3

--- a/solution.py
+++ b/solution.py
@@ -44,9 +44,9 @@
 
 def kernel(
     sizes,
-    band_ref,
     lat_ref,
     lon_ref,
+    band_hbm,
     tok_hbm,
     gout_hbm,
     wqkv_hbm,
@@ -55,10 +55,10 @@
     gw_ref,
     wqkv,
     wout,
+    band_ref,
+    own_block,
     tok_wide,
     gout_wide,
-    tok_rows,
-    gout_rows,
     lat_send,
     xo,
     xg,
@@ -88,8 +88,6 @@
     load_sem,
     halo_send_sem,
     halo_recv_sem,
-    lat_send_sem,
-    lat_recv_sem,
     core_send_sem,
     core_recv_sem,
     xg_send_sem,
@@ -121,6 +119,8 @@
     right = ((lon + 1) % n_lon, lat, core)
     left = ((lon + n_lon - 1) % n_lon, lat, core)
     across = (lon, (lat + 1) % n_lat, core)
+    across_right = ((lon + 1) % n_lon, (lat + 1) % n_lat, core)
+    across_left = ((lon + n_lon - 1) % n_lon, (lat + 1) % n_lat, core)
     sibling = (lon, lat, 1 - core)
 
     def x_peer(d):
@@ -157,7 +157,7 @@
     def slim_block(i):
         return either(y_block(i), x_block(i))
 
-    partners = [right, left, across, sibling]
+    partners = [right, left, across, across_right, across_left, sibling]
     partners += [x_peer(d) for d in range(1, NX)]
     partners += [y_peer(d) for d in range(1, n_y)]
     partners += [z_peer(d) for d in range(1, NZ)]
@@ -176,15 +176,19 @@
     for partner in partners:
         pl.semaphore_signal(barrier, inc=1, device_id=partner, device_id_type=MESH)
 
+    load_band = pltpu.make_async_copy(band_hbm, band_ref, load_sem.at[0])
+    load_band.start()
     inputs = (tok_hbm, gout_hbm)
     wides = (tok_wide, gout_wide)
-    rows_of = (tok_rows, gout_rows)
+    middle = slice(HALF_COLS, HALF_COLS + WLON)
     loads = []
     for a in range(2):
-        middle = wides[a].at[:, HALF_COLS : HALF_COLS + WLON]
-        loads.append(pltpu.make_async_copy(inputs[a], middle, load_sem.at[a]))
-    loads.append(pltpu.make_async_copy(wqkv_hbm, wqkv, load_sem.at[2]))
-    loads.append(pltpu.make_async_copy(wout_hbm, wout, load_sem.at[3]))
+        loads.append(pltpu.make_async_copy(inputs[a], own_block.at[a], load_sem.at[1 + a]))
+        loads.append(
+            pltpu.make_async_copy(inputs[a], wides[a].at[0:WLAT, middle], load_sem.at[3 + a])
+        )
+    loads.append(pltpu.make_async_copy(wqkv_hbm, wqkv, load_sem.at[5]))
+    loads.append(pltpu.make_async_copy(wout_hbm, wout, load_sem.at[6]))
     for load in loads:
         load.start()
 
@@ -195,6 +199,12 @@
     f = row_shift - WLAT * row_swap
     e = col_shift - WLON * col_swap
 
+    loads[0].wait()
+    loads[2].wait()
+    for a in range(2):
+        lat_send[a] = own_block[a, pl.ds(HALF_ROWS * row_swap, HALF_ROWS)]
+
+    load_band.wait()
     k_at = iota((TOK, TOK), 0)
     q_at = iota((TOK, TOK), 1)
     first_row = WLAT * ((lat + row_swap) % n_lat) + row_shift
@@ -216,54 +226,42 @@
     pl.semaphore_wait(barrier, len(partners))
 
     halo = []
+    before = slice(0, HALF_COLS)
+    after = slice(HALF_COLS + WLON, 2 * WLON)
+    left_half = slice(0, HALF_COLS)
+    right_half = slice(HALF_COLS, WLON)
+    kept = slice(0, WLAT)
+    borrowed = slice(WLAT, WLAT + HALF_ROWS)
     for a in range(2):
-        to_left = remote(
-            inputs[a].at[:, 0:HALF_COLS],
-            wides[a].at[:, HALF_COLS + WLON : 2 * WLON],
-            halo_send_sem.at[a, 0],
-            halo_recv_sem.at[a, 0],
-            left,
-        )
-        to_right = remote(
-            inputs[a].at[:, HALF_COLS:WLON],
-            wides[a].at[:, 0:HALF_COLS],
-            halo_send_sem.at[a, 1],
-            halo_recv_sem.at[a, 1],
-            right,
-        )
-        to_left.start()
-        to_right.start()
-        halo.append((to_left, to_right))
-
-    sends = [copy for pair in halo for copy in pair]
-    over_lat = []
+        copies = []
+        for n, (src, rows, columns, device) in enumerate(
+            (
+                (lat_send.at[a], borrowed, middle, across),
+                (inputs[a].at[:, left_half], kept, after, left),
+                (inputs[a].at[:, right_half], kept, before, right),
+                (lat_send.at[a, :, left_half], borrowed, after, across_left),
+                (lat_send.at[a, :, right_half], borrowed, before, across_right),
+            )
+        ):
+            copy = remote(
+                src, wides[a].at[rows, columns], halo_send_sem.at[a, n], halo_recv_sem.at[a, n], device
+            )
+            copy.start()
+            copies.append(copy)
+        halo.append(copies)
+    sends = [copy for copies in halo for copy in copies]
+
+    over_core = []
+    over_plane = {}
     for a in range(2):
-        loads[a].wait()
+        loads[2 * a + 1].wait()
         for copy in halo[a]:
             copy.wait_recv()
         columns = pl.ds(e + HALF_COLS, WLON)
-        lat_send[a] = wides[a][pl.ds(HALF_ROWS * row_swap, HALF_ROWS), columns]
-        copy = remote(
-            lat_send.at[a],
-            rows_of[a].at[WLAT : WLAT + HALF_ROWS],
-            lat_send_sem.at[a],
-            lat_recv_sem.at[a],
-            across,
-        )
-        copy.start()
-        over_lat.append(copy)
-        rows_of[a][0:WLAT] = wides[a][:, columns]
-    sends += over_lat
-
-    over_core = []
-    over_plane = {}
-    for a in range(2):
-        over_lat[a].wait_recv()
         picked = []
         for r in range(WLAT):
             q = f + r
-            place = jnp.where(q < 0, q + (WLAT + HALF_ROWS), q)
-            picked.append(rows_of[a][place])
+            picked.append(wides[a][jnp.where(q < 0, q + (WLAT + HALF_ROWS), q), columns])
         window = jnp.stack(picked).reshape(TOK, half)
         if a == 0:
             xo[core] = window
@@ -288,12 +286,12 @@
                     over_plane[axis, d] = copy
     sends += over_core + list(over_plane.values())
 
-    loads[2].wait()
+    loads[4].wait()
     over_core[0].wait_recv()
     for j in range(3):
         total = nn(xo[0], wqkv[j, :half]) + nn(xo[1], wqkv[j, half:])
         qkv[j] = total.astype(BF16)
-    loads[3].wait()
+    loads[5].wait()
     over_core[1].wait_recv()
     ga[...] = (nt(go[0], wout[:, :half]) + nt(go[1], wout[:, half:])).astype(BF16)
 
@@ -302,6 +300,18 @@
 
     def sum_peer(t, d):
         return slim_peer(d) if t < 2 else wide_peer(d)
+
+    relays = {}
+
+    def relay(d):
+        for axis in range(2):
+            over_plane[axis, d].wait_recv()
+            mine = xg.at[axis, d, core]
+            copy = remote(
+                mine, mine, relay_send_sem.at[axis, d], relay_recv_sem.at[axis, d], sibling
+            )
+            copy.start()
+            relays[axis, d] = copy
 
     scale = HEAD_DIM ** (-0.5)
     over_g = {}
@@ -335,6 +345,10 @@
                 )
                 copy.start()
                 over_g[t, d] = copy
+        if t == 0:
+            for d in range(1, NX):
+                if d != NX // 2:
+                    relay(d)
     for d in range(1, NX):
         copy = remote(
             gall.at[2, (slim_at + d) % NX],
@@ -345,44 +359,8 @@
         )
         copy.start()
         over_g[2, d] = copy
-    sends += list(over_g.values())
-
-    def grad_in(which):
-        rows = pl.ds(pl.multiple_of(which * half, half), half)
-        total = 0.0
-        for j in range(3):
-            joined = jnp.concatenate([gall[j, pair] for pair in range(NX)], 1)
-            total = total + nt(joined, wqkv[j, rows])
-        return total
-
-    gin[0] = grad_in(1 - core)
-    to_sibling = remote(gin.at[0], gin_recv, core_send_sem.at[2], core_recv_sem.at[2], sibling)
-    to_sibling.start()
-    relays = {}
-    for key, copy in over_plane.items():
-        axis, d = key
-        copy.wait_recv()
-        mine = xg.at[axis, d, core]
-        relay = remote(mine, mine, relay_send_sem.at[axis, d], relay_recv_sem.at[axis, d], sibling)
-        relay.start()
-        relays[key] = relay
-    gin[1] = grad_in(core)
-
-    to_sibling.wait_recv()
-    window = (gin[1] + gin_recv[...]).astype(BF16).reshape(WLAT, WLON, LEV, half)
-    back_own[...] = window
-    back_rows[0:WLAT] = window
-    for k in range(HALF_ROWS):
-        from_row = k + jnp.where(f > 0, WLAT, -HALF_ROWS) - f
-        back_send[k] = back_own[jnp.clip(from_row, 0, WLAT - 1)]
-    over_lat_back = remote(
-        back_send,
-        back_rows.at[WLAT : WLAT + HALF_ROWS],
-        lat_send_sem.at[2],
-        lat_recv_sem.at[2],
-        across,
-    )
-    over_lat_back.start()
+    relay(NX // 2)
+    sends += list(over_g.values()) + list(relays.values())
 
     blocks = parts.shape[1]
     own = parts.shape[2]
@@ -429,33 +407,34 @@
             over_p[t, d] = copy
     sends += list(over_p.values())
 
-    over_lat_back.wait_recv()
-    for b in range(WLAT):
-        was = b - f
-        home = (was >= 0) & (was < WLAT)
-        row = back_rows[jnp.where(home, was, b + WLAT - HALF_ROWS * row_swap)]
-        side_own[b] = row
-        side_cols[b, 0:WLON] = row
-    for s in range(HALF_COLS):
-        side_send[0, :, s] = side_own[:, jnp.clip(s - HALF_COLS - e, 0, WLON - 1)]
-        side_send[1, :, s] = side_own[:, jnp.clip(s + WLON - e, 0, WLON - 1)]
-    side_left = remote(
-        side_send.at[0],
-        side_cols.at[:, WLON + HALF_COLS : 2 * WLON],
+    def grad_in(which):
+        rows = pl.ds(pl.multiple_of(which * half, half), half)
+        total = 0.0
+        for j in range(3):
+            joined = jnp.concatenate([gall[j, pair] for pair in range(NX)], 1)
+            total = total + nt(joined, wqkv[j, rows])
+        return total
+
+    gin[0] = grad_in(1 - core)
+    to_sibling = remote(gin.at[0], gin_recv, core_send_sem.at[2], core_recv_sem.at[2], sibling)
+    to_sibling.start()
+    gin[1] = grad_in(core)
+
+    to_sibling.wait_recv()
+    window = (gin[1] + gin_recv[...]).astype(BF16).reshape(WLAT, WLON, LEV, half)
+    back_own[...] = window
+    back_rows[0:WLAT] = window
+    for k in range(HALF_ROWS):
+        from_row = k + jnp.where(f > 0, WLAT, -HALF_ROWS) - f
+        back_send[k] = back_own[jnp.clip(from_row, 0, WLAT - 1)]
+    over_lat_back = remote(
+        back_send,
+        back_rows.at[WLAT : WLAT + HALF_ROWS],
         halo_send_sem.at[2, 0],
         halo_recv_sem.at[2, 0],
-        left,
+        across,
     )
-    side_right = remote(
-        side_send.at[1],
-        side_cols.at[:, WLON : WLON + HALF_COLS],
-        halo_send_sem.at[2, 1],
-        halo_recv_sem.at[2, 1],
-        right,
-    )
-    side_left.start()
-    side_right.start()
-    sends += [to_sibling, over_lat_back, side_left, side_right] + list(relays.values())
+    over_lat_back.start()
 
     over_z = {}
     for t in range(3):
@@ -476,6 +455,34 @@
             copy.start()
             over_z[t, d] = copy
     sends += list(over_z.values())
+
+    over_lat_back.wait_recv()
+    for b in range(WLAT):
+        was = b - f
+        home = (was >= 0) & (was < WLAT)
+        row = back_rows[jnp.where(home, was, b + WLAT - HALF_ROWS * row_swap)]
+        side_own[b] = row
+        side_cols[b, 0:WLON] = row
+    for s in range(HALF_COLS):
+        side_send[0, :, s] = side_own[:, jnp.clip(s - HALF_COLS - e, 0, WLON - 1)]
+        side_send[1, :, s] = side_own[:, jnp.clip(s + WLON - e, 0, WLON - 1)]
+    side_left = remote(
+        side_send.at[0],
+        side_cols.at[:, WLON + HALF_COLS : 2 * WLON],
+        halo_send_sem.at[2, 1],
+        halo_recv_sem.at[2, 1],
+        left,
+    )
+    side_right = remote(
+        side_send.at[1],
+        side_cols.at[:, WLON : WLON + HALF_COLS],
+        halo_send_sem.at[2, 2],
+        halo_recv_sem.at[2, 2],
+        right,
+    )
+    side_left.start()
+    side_right.start()
+    sends += [to_sibling, over_lat_back, side_left, side_right]
 
     side_left.wait_recv()
     side_right.wait_recv()
@@ -540,18 +547,18 @@
         gtok, gw = pl.pallas_call(
             functools.partial(kernel, (n_lon, n_lat, width, half)),
             out_shape=(
-                jax.ShapeDtypeStruct((WLAT, WLON, LEV, half), BF16),
-                jax.ShapeDtypeStruct((3, own, half), F32),
+                pltpu.VMEM((WLAT, WLON, LEV, half), BF16),
+                pltpu.VMEM((3, own, half), F32),
             ),
-            in_specs=[smem, smem, smem, hbm, hbm, hbm, hbm],
+            in_specs=[smem] * 2 + [hbm] * 5,
             out_specs=(vmem, vmem),
             scratch_shapes=[
                 pltpu.VMEM((3, width, half), BF16),
                 pltpu.VMEM((half, width), BF16),
-                pltpu.VMEM((WLAT, 2 * WLON, LEV, half), BF16),
-                pltpu.VMEM((WLAT, 2 * WLON, LEV, half), BF16),
-                pltpu.VMEM((WLAT + HALF_ROWS, WLON, LEV, half), BF16),
-                pltpu.VMEM((WLAT + HALF_ROWS, WLON, LEV, half), BF16),
+                pltpu.SMEM(band_count.shape, jnp.int32),
+                pltpu.VMEM((2, WLAT, WLON, LEV, half), BF16),
+                pltpu.VMEM((WLAT + HALF_ROWS, 2 * WLON, LEV, half), BF16),
+                pltpu.VMEM((WLAT + HALF_ROWS, 2 * WLON, LEV, half), BF16),
                 pltpu.VMEM((2, HALF_ROWS, WLON, LEV, half), BF16),
                 pltpu.VMEM((2, TOK, half), BF16),
                 pltpu.VMEM((2, NX, 2, TOK, half), BF16),
@@ -578,11 +585,9 @@
                 pltpu.VMEM((3, NZ, NX * own, cut), BF16),
                 pltpu.VMEM((NX, 3, own, cut), F32),
                 pltpu.VMEM((NX, 3, own, cut), F32),
-                dma((4,)),
-                dma((3, 2)),
-                dma((3, 2)),
-                dma((3,)),
-                dma((3,)),
+                dma((7,)),
+                dma((3, 5)),
+                dma((3, 5)),
                 dma((3,)),
                 dma((3,)),
                 dma((2, NX)),
@@ -602,13 +607,18 @@
                 collective_id=0, has_side_effects=True, vmem_limit_bytes=60 * 2**20
             ),
         )(
-            band_count,
             lat_shift,
             lon_shift,
-            tokens.transpose(1, 2, 0, 3),
-            grad_out.transpose(1, 2, 0, 3),
-            w_qkv,
-            w_out,
+            *(
+                pltpu.with_memory_space_constraint(array, pltpu.HBM)
+                for array in (
+                    band_count,
+                    tokens.transpose(1, 2, 0, 3),
+                    grad_out.transpose(1, 2, 0, 3),
+                    w_qkv,
+                    w_out,
+                )
+            )
         )
         return gtok.transpose(2, 0, 1, 3), gw
 

time: 55.9 us -> 55.3 us (0.989)
  local copies, waits for them, and re-layouts: 3.09 us -> 1.28 us
  Pallas kernels: 50.6 us -> 52 us
    unnamed x2, local copies, waits for them, and re-layouts: 3.09 us -> 1.28 us
    pallas_call x1, Pallas kernels: 50.6 us -> 52 us  [shards(): pl.pallas_call(functools.partial(kernel, (n_lon, n_lat, width, half)), ou...]
where the time goes in v4:
time: 55.3 us; the launch traced here: 55.2 us
  Pallas kernels  52 us (94%)
  between operations  1.93 us (3%)
  local copies, waits for them, and re-layouts  1.28 us (2%)
    pallas_call x1, Pallas kernels, shards(): pl.pallas_call(functools.partial(kernel, (n_lon, n_lat, width, half)), ou...  52 us
    unnamed x2, local copies, waits for them, and re-layouts  1.28 us

profile of v4, /device:TPU:1, one launch (start us, length us, event | category | flops | bytes accessed | tf_op | source)
XLA Modules:
  0.0 55.2 jit_solution(11828156964397915379)
XLA Ops:
  1.9 52.0 %shard_map.86 = (bf16[12,6,2,512]{3,2,1,0:T(2,128)(2,1)S(1)}, f32[3,8,512]{2,1,0:T(8,128)S(1)}) custom-call(s32[1]{0:T(128)S(6)} %copy.13.lat_ref, s32[1]{0:T(128)S(6)} %copy.14.lon_ref, s32[24]{0:T(128)} %band_hbm.1, bf16[12,6,2,512]{3,2,1,0:T(2,128)(2,1)} %bitcast.4, bf16[12,6,2,512]{3,2,1,0:T(2,128)(2,1)} %bitcast.5, bf16[3,1024,512]{2,1,0:T(8,128)(2,1)} %wqkv_hbm.1, ...), custom_call_target="tpu_custom_call" | custom-call | tf_op jit(solution)/shard_map/pallas_call | solution.py:547
  53.9 0.7 %copy.11 = bf16[2,12,6,512]{3,0,2,1:T(2,128)(2,1)} copy(bf16[2,12,6,512]{3,0,2,1:T(2,128)(2,1)S(1)} %bitcast.3) | data formatting | bytes 294912
  54.6 0.6 %copy.12 = f32[3,8,512]{2,1,0:T(8,128)} copy(f32[3,8,512]{2,1,0:T(8,128)S(1)} %get-tuple-element.7) | data formatting | bytes 98304

commit v5 on v4

--- a/solution.py
+++ b/solution.py
@@ -64,6 +64,7 @@
     xg,
     go,
     bias,
+    probs_of,
     qkv,
     ga,
     gall,
@@ -253,7 +254,8 @@
 
     over_core = []
     over_plane = {}
-    for a in range(2):
+
+    def make_window(a):
         loads[2 * a + 1].wait()
         for copy in halo[a]:
             copy.wait_recv()
@@ -262,35 +264,52 @@
         for r in range(WLAT):
             q = f + r
             picked.append(wides[a][jnp.where(q < 0, q + (WLAT + HALF_ROWS), q), columns])
-        window = jnp.stack(picked).reshape(TOK, half)
-        if a == 0:
-            xo[core] = window
-            mine = xo.at[core]
-        else:
-            go[core] = window
-            mine = go.at[core]
+        held = (xo, go)[a]
+        held[core] = jnp.stack(picked).reshape(TOK, half)
+        mine = held.at[core]
         copy = remote(mine, mine, core_send_sem.at[a], core_recv_sem.at[a], sibling)
         copy.start()
         over_core.append(copy)
-        if a == 0:
-            for d in range(1, NX):
-                for axis, peer in ((0, x_peer(d)), (1, y_peer(d))):
-                    copy = remote(
-                        xo.at[core],
-                        xg.at[axis, d, core],
-                        xg_send_sem.at[axis, d],
-                        xg_recv_sem.at[axis, d],
-                        peer,
-                    )
-                    copy.start()
-                    over_plane[axis, d] = copy
-    sends += over_core + list(over_plane.values())
+
+    make_window(0)
+    for d in (1, NX - 1) + tuple(range(2, NX - 1)):
+        for axis, peer in ((0, x_peer(d)), (1, y_peer(d))):
+            if (axis, d) in over_plane:
+                continue
+            copy = remote(
+                xo.at[core],
+                xg.at[axis, d, core],
+                xg_send_sem.at[axis, d],
+                xg_recv_sem.at[axis, d],
+                peer,
+            )
+            copy.start()
+            over_plane[axis, d] = copy
+    sends += list(over_plane.values())
 
     loads[4].wait()
     over_core[0].wait_recv()
     for j in range(3):
         total = nn(xo[0], wqkv[j, :half]) + nn(xo[1], wqkv[j, half:])
         qkv[j] = total.astype(BF16)
+
+    scale = HEAD_DIM ** (-0.5)
+    order = []
+    for t in range(2):
+        at = slice(t * HEAD_DIM, (t + 1) * HEAD_DIM)
+        for n in range(NX):
+            d = (n + 1) % NX
+            pair = (wide_at + d) % NX
+            lanes = pl.ds(pl.multiple_of(pair * cut, cut), cut)
+            order.append((t, at, d, pair, lanes))
+    for n, (t, at, d, pair, lanes) in enumerate(order):
+        scores = nt(qkv[1, :, lanes][:, at], qkv[0, :, lanes][:, at]) * scale
+        scores = jnp.where(bias[...] == 0.0, scores, -1e30)
+        raised = jnp.exp(scores - jnp.max(scores, 0, keepdims=True))
+        probs_of[n] = raised * (1.0 / jnp.sum(raised, 0, keepdims=True))
+
+    make_window(1)
+    sends += over_core
     loads[5].wait()
     over_core[1].wait_recv()
     ga[...] = (nt(go[0], wout[:, :half]) + nt(go[1], wout[:, half:])).astype(BF16)
@@ -313,42 +332,30 @@
             copy.start()
             relays[axis, d] = copy
 
-    scale = HEAD_DIM ** (-0.5)
     over_g = {}
-    for t in range(2):
-        at = slice(t * HEAD_DIM, (t + 1) * HEAD_DIM)
-        for n in range(NX):
-            d = (n + 1) % NX
-            pair = (wide_at + d) % NX
-            lanes = pl.ds(pl.multiple_of(pair * cut, cut), cut)
-            q, k, v = (qkv[j, :, lanes][:, at] for j in range(3))
-            g = ga[:, lanes][:, at]
-            scores = jnp.where(bias[...] == 0.0, nt(k, q) * scale, -1e30)
-            raised = jnp.exp(scores - jnp.max(scores, 0, keepdims=True))
-            probs = raised * (1.0 / jnp.sum(raised, 0, keepdims=True))
-            grad_probs = nt(v, g)
-            inner = jnp.sum(probs * grad_probs, 0, keepdims=True)
-            grad_scores = (probs * (grad_probs - inner) * scale).astype(BF16)
-            grad_q = tn(grad_scores, k).astype(BF16)
-            grad_k = nn(grad_scores, q).astype(BF16)
-            gall[0, pair, :, at] = grad_q
-            gall[1, pair, :, at] = grad_k
-            gall[2, pair, :, at] = nn(probs.astype(BF16), g).astype(BF16)
-            own_qk[t, d] = jnp.concatenate([grad_q, grad_k], 1)
-            if d:
-                copy = remote(
-                    own_qk.at[t, d],
-                    g_recv.at[t, d],
-                    g_send_sem.at[t, d],
-                    g_recv_sem.at[t, d],
-                    factor_peer(t, d),
-                )
-                copy.start()
-                over_g[t, d] = copy
-        if t == 0:
-            for d in range(1, NX):
-                if d != NX // 2:
-                    relay(d)
+    for n, (t, at, d, pair, lanes) in enumerate(order):
+        q, k, v = (qkv[j, :, lanes][:, at] for j in range(3))
+        g = ga[:, lanes][:, at]
+        probs = probs_of[n]
+        grad_probs = nt(v, g)
+        inner = jnp.sum(probs * grad_probs, 0, keepdims=True)
+        grad_scores = (probs * (grad_probs - inner) * scale).astype(BF16)
+        grad_q = tn(grad_scores, k).astype(BF16)
+        grad_k = nn(grad_scores, q).astype(BF16)
+        gall[0, pair, :, at] = grad_q
+        gall[1, pair, :, at] = grad_k
+        gall[2, pair, :, at] = nn(probs.astype(BF16), g).astype(BF16)
+        own_qk[t, d] = jnp.concatenate([grad_q, grad_k], 1)
+        if d:
+            copy = remote(
+                own_qk.at[t, d],
+                g_recv.at[t, d],
+                g_send_sem.at[t, d],
+                g_recv_sem.at[t, d],
+                factor_peer(t, d),
+            )
+            copy.start()
+            over_g[t, d] = copy
     for d in range(1, NX):
         copy = remote(
             gall.at[2, (slim_at + d) % NX],
@@ -359,8 +366,23 @@
         )
         copy.start()
         over_g[2, d] = copy
-    relay(NX // 2)
-    sends += list(over_g.values()) + list(relays.values())
+    sends += list(over_g.values())
+
+    def grad_in(which):
+        rows = pl.ds(pl.multiple_of(which * half, half), half)
+        total = 0.0
+        for j in range(3):
+            joined = jnp.concatenate([gall[j, pair] for pair in range(NX)], 1)
+            total = total + nt(joined, wqkv[j, rows])
+        return total
+
+    gin[0] = grad_in(1 - core)
+    to_sibling = remote(gin.at[0], gin_recv, core_send_sem.at[2], core_recv_sem.at[2], sibling)
+    to_sibling.start()
+    for d in (1, NX - 1) + tuple(range(2, NX - 1)):
+        if (0, d) not in relays:
+            relay(d)
+    sends += list(relays.values())
 
     blocks = parts.shape[1]
     own = parts.shape[2]
@@ -407,17 +429,6 @@
             over_p[t, d] = copy
     sends += list(over_p.values())
 
-    def grad_in(which):
-        rows = pl.ds(pl.multiple_of(which * half, half), half)
-        total = 0.0
-        for j in range(3):
-            joined = jnp.concatenate([gall[j, pair] for pair in range(NX)], 1)
-            total = total + nt(joined, wqkv[j, rows])
-        return total
-
-    gin[0] = grad_in(1 - core)
-    to_sibling = remote(gin.at[0], gin_recv, core_send_sem.at[2], core_recv_sem.at[2], sibling)
-    to_sibling.start()
     gin[1] = grad_in(core)
 
     to_sibling.wait_recv()
@@ -564,6 +575,7 @@
                 pltpu.VMEM((2, NX, 2, TOK, half), BF16),
                 pltpu.VMEM((2, TOK, half), BF16),
                 pltpu.VMEM((TOK, TOK), F32),
+                pltpu.VMEM((half // HEAD_DIM, TOK, TOK), F32),
                 pltpu.VMEM((3, TOK, half), BF16),
                 pltpu.VMEM((TOK, half), BF16),
                 pltpu.VMEM((3, NX, TOK, cut), BF16),

time: 55.3 us -> 53.6 us (0.969)
  Pallas kernels: 52 us -> 50.3 us
    pallas_call x1, Pallas kernels: 52 us -> 50.3 us  [shards(): pl.pallas_call(functools.partial(kernel, (n_lon, n_lat, width, half)), ou...]
where the time goes in v5:
time: 53.6 us; the launch traced here: 53.5 us
  Pallas kernels  50.3 us (94%)
  between operations  1.93 us (4%)
  local copies, waits for them, and re-layouts  1.28 us (2%)
    pallas_call x1, Pallas kernels, shards(): pl.pallas_call(functools.partial(kernel, (n_lon, n_lat, width, half)), ou...  50.3 us
    unnamed x2, local copies, waits for them, and re-layouts  1.28 us

profile of v5, /device:TPU:1, one launch (start us, length us, event | category | flops | bytes accessed | tf_op | source)
XLA Modules:
  0.0 53.5 jit_solution(15734356945423964264)
XLA Ops:
  1.9 50.3 %shard_map.86 = (bf16[12,6,2,512]{3,2,1,0:T(2,128)(2,1)S(1)}, f32[3,8,512]{2,1,0:T(8,128)S(1)}) custom-call(s32[1]{0:T(128)S(6)} %copy.13.lat_ref, s32[1]{0:T(128)S(6)} %copy.14.lon_ref, s32[24]{0:T(128)} %band_hbm.1, bf16[12,6,2,512]{3,2,1,0:T(2,128)(2,1)} %bitcast.4, bf16[12,6,2,512]{3,2,1,0:T(2,128)(2,1)} %bitcast.5, bf16[3,1024,512]{2,1,0:T(8,128)(2,1)} %wqkv_hbm.1, ...), custom_call_target="tpu_custom_call" | custom-call | tf_op jit(solution)/shard_map/pallas_call | solution.py:558
  52.3 0.7 %copy.11 = bf16[2,12,6,512]{3,0,2,1:T(2,128)(2,1)} copy(bf16[2,12,6,512]{3,0,2,1:T(2,128)(2,1)S(1)} %bitcast.3) | data formatting | bytes 294912
  52.9 0.6 %copy.12 = f32[3,8,512]{2,1,0:T(8,128)} copy(f32[3,8,512]{2,1,0:T(8,128)S(1)} %get-tuple-element.7) | data formatting | bytes 98304

commit v6 on v5

--- a/solution.py
+++ b/solution.py
@@ -379,55 +379,17 @@
     gin[0] = grad_in(1 - core)
     to_sibling = remote(gin.at[0], gin_recv, core_send_sem.at[2], core_recv_sem.at[2], sibling)
     to_sibling.start()
+    blocks = parts.shape[1]
+    own = parts.shape[2]
+    sides = [slice(0, blocks // 2), slice(blocks // 2, blocks)]
+    for t in range(3):
+        for side, rows in enumerate(sides):
+            product = tn(xo[side], own_qk[t, 0] if t < 2 else gall[2, slim_at])
+            parts[t, rows] = product.reshape(blocks // 2, own, cut)
     for d in (1, NX - 1) + tuple(range(2, NX - 1)):
         if (0, d) not in relays:
             relay(d)
     sends += list(relays.values())
-
-    blocks = parts.shape[1]
-    own = parts.shape[2]
-
-    def make_product(t):
-        axis = core if t < 2 else 1 - core
-        halves = []
-        for side in range(2):
-            halves.append(tn(xo[side], own_qk[t, 0] if t < 2 else gall[2, slim_at]))
-        for d in range(1, NX):
-            if t == 0:
-                relays[0, d].wait_recv()
-                relays[1, d].wait_recv()
-            over_g[t, d].wait_recv()
-            for side in range(2):
-                halves[side] = halves[side] + tn(xg[axis, d, side], g_recv[t, d])
-        for side in range(2):
-            rows = slice(side * (blocks // 2), (side + 1) * (blocks // 2))
-            parts[t, rows] = halves[side].reshape(blocks // 2, own, cut)
-
-    def owner_rows(t, i):
-        base = slim_block(i) if t < 2 else wide_block(i)
-        picked = []
-        for k in range(NZ):
-            for j in range(NX):
-                along = wide_block(j) if t < 2 else slim_block(j)
-                picked.append(parts[t, base + along + k * (NX * n_lat)])
-        return jnp.concatenate(picked, 0)
-
-    over_p = {}
-    for t in range(3):
-        make_product(t)
-        place = slim_at if t < 2 else wide_at
-        for d in range(1, NX):
-            psend[t, d] = owner_rows(t, (place + d) % NX).astype(BF16)
-            copy = remote(
-                psend.at[t, d],
-                precv.at[t, d],
-                p_send_sem.at[t, d],
-                p_recv_sem.at[t, d],
-                sum_peer(t, d),
-            )
-            copy.start()
-            over_p[t, d] = copy
-    sends += list(over_p.values())
 
     gin[1] = grad_in(core)
 
@@ -447,25 +409,43 @@
     )
     over_lat_back.start()
 
-    over_z = {}
+    def make_product(t):
+        axis = core if t < 2 else 1 - core
+        halves = [parts[t, rows].reshape(half, cut) for rows in sides]
+        for d in range(1, NX):
+            if t == 0:
+                relays[0, d].wait_recv()
+                relays[1, d].wait_recv()
+            over_g[t, d].wait_recv()
+            for side in range(2):
+                halves[side] = halves[side] + tn(xg[axis, d, side], g_recv[t, d])
+        for side, rows in enumerate(sides):
+            parts[t, rows] = halves[side].reshape(blocks // 2, own, cut)
+
+    def owner_rows(t, i):
+        base = slim_block(i) if t < 2 else wide_block(i)
+        picked = []
+        for k in range(NZ):
+            for j in range(NX):
+                along = wide_block(j) if t < 2 else slim_block(j)
+                picked.append(parts[t, base + along + k * (NX * n_lat)])
+        return jnp.concatenate(picked, 0)
+
+    over_p = {}
     for t in range(3):
-        total = owner_rows(t, slim_at if t < 2 else wide_at)
+        make_product(t)
+        place = slim_at if t < 2 else wide_at
         for d in range(1, NX):
-            over_p[t, d].wait_recv()
-            total = total + precv[t, d].astype(F32)
-        rz[t] = total.reshape(NZ, NX * own, cut)
-        for d in range(1, NZ):
-            zsend[t, d] = rz[t, (z + d) % NZ].astype(BF16)
+            psend[t, d] = owner_rows(t, (place + d) % NX).astype(BF16)
             copy = remote(
-                zsend.at[t, d],
-                zrecv.at[t, d],
-                z_send_sem.at[t, d],
-                z_recv_sem.at[t, d],
-                z_peer(d),
+                psend.at[t, d],
+                precv.at[t, d],
+                p_send_sem.at[t, d],
+                p_recv_sem.at[t, d],
+                sum_peer(t, d),
             )
             copy.start()
-            over_z[t, d] = copy
-    sends += list(over_z.values())
+            over_p[t, d] = copy
 
     over_lat_back.wait_recv()
     for b in range(WLAT):
@@ -493,7 +473,30 @@
     )
     side_left.start()
     side_right.start()
-    sends += [to_sibling, over_lat_back, side_left, side_right]
+
+    for copy in sends:
+        copy.wait_send()
+
+    over_z = {}
+    for t in range(3):
+        total = owner_rows(t, slim_at if t < 2 else wide_at)
+        for d in range(1, NX):
+            over_p[t, d].wait_recv()
+            total = total + precv[t, d].astype(F32)
+        rz[t] = total.reshape(NZ, NX * own, cut)
+        for d in range(1, NZ):
+            zsend[t, d] = rz[t, (z + d) % NZ].astype(BF16)
+            copy = remote(
+                zsend.at[t, d],
+                zrecv.at[t, d],
+                z_send_sem.at[t, d],
+                z_recv_sem.at[t, d],
+                z_peer(d),
+            )
+            copy.start()
+            over_z[t, d] = copy
+    for copy in list(over_p.values()) + [to_sibling, over_lat_back, side_left, side_right]:
+        copy.wait_send()
 
     side_left.wait_recv()
     side_right.wait_recv()
@@ -523,7 +526,6 @@
             )
             copy.start()
             last[t, d] = copy
-    sends += list(last.values())
     for d in range(NX):
         if d:
             last[1, d].wait_recv()
@@ -538,7 +540,7 @@
         lanes = pl.ds(pl.multiple_of(((slim_at + NX - d) % NX) * cut, cut), cut)
         gw_ref[2, :, lanes] = values
 
-    for copy in sends:
+    for copy in list(over_z.values()) + list(last.values()):
         copy.wait_send()
 
 

time: 53.6 us -> 52 us (0.970)
  Pallas kernels: 50.3 us -> 48.7 us
    pallas_call x1, Pallas kernels: 50.3 us -> 48.7 us  [shards(): pl.pallas_call(functools.partial(kernel, (n_lon, n_lat, width, half)), ou...]
where the time goes in v6:
time: 52 us; the launch traced here: 51.9 us
  Pallas kernels  48.7 us (94%)
  between operations  1.93 us (4%)
  local copies, waits for them, and re-layouts  1.28 us (2%)
    pallas_call x1, Pallas kernels, shards(): pl.pallas_call(functools.partial(kernel, (n_lon, n_lat, width, half)), ou...  48.7 us
    unnamed x2, local copies, waits for them, and re-layouts  1.28 us

profile of v6, /device:TPU:1, one launch (start us, length us, event | category | flops | bytes accessed | tf_op | source)
XLA Modules:
  0.0 51.9 jit_solution(910022453388490103)
XLA Ops:
  1.9 48.7 %shard_map.86 = (bf16[12,6,2,512]{3,2,1,0:T(2,128)(2,1)S(1)}, f32[3,8,512]{2,1,0:T(8,128)S(1)}) custom-call(s32[1]{0:T(128)S(6)} %copy.13.lat_ref, s32[1]{0:T(128)S(6)} %copy.14.lon_ref, s32[24]{0:T(128)} %band_hbm.1, bf16[12,6,2,512]{3,2,1,0:T(2,128)(2,1)} %bitcast.4, bf16[12,6,2,512]{3,2,1,0:T(2,128)(2,1)} %bitcast.5, bf16[3,1024,512]{2,1,0:T(8,128)(2,1)} %wqkv_hbm.1, ...), custom_call_target="tpu_custom_call" | custom-call | tf_op jit(solution)/shard_map/pallas_call | solution.py:560
  50.7 0.7 %copy.11 = bf16[2,12,6,512]{3,0,2,1:T(2,128)(2,1)} copy(bf16[2,12,6,512]{3,0,2,1:T(2,128)(2,1)S(1)} %bitcast.3) | data formatting | bytes 294912
  51.3 0.6 %copy.12 = f32[3,8,512]{2,1,0:T(8,128)} copy(f32[3,8,512]{2,1,0:T(8,128)S(1)} %get-tuple-element.7) | data formatting | bytes 98304

commit v7 on v6

--- a/solution.py
+++ b/solution.py
@@ -134,6 +134,9 @@
     def z_peer(d):
         return (lon + ((z + d) % NZ - z) * NX, lat, core)
 
+    far_x = sorted(range(1, NX), key=lambda d: -min(d, NX - d))
+    far_z = sorted(range(1, NZ), key=lambda d: -min(d, NZ - d))
+
     def either(for_first, for_second):
         return for_first + core * (for_second - for_first)
 
@@ -188,10 +191,10 @@
         loads.append(
             pltpu.make_async_copy(inputs[a], wides[a].at[0:WLAT, middle], load_sem.at[3 + a])
         )
+    for load in loads:
+        load.start()
     loads.append(pltpu.make_async_copy(wqkv_hbm, wqkv, load_sem.at[5]))
     loads.append(pltpu.make_async_copy(wout_hbm, wout, load_sem.at[6]))
-    for load in loads:
-        load.start()
 
     row_shift = lat_ref[0]
     col_shift = lon_ref[0]
@@ -200,10 +203,47 @@
     f = row_shift - WLAT * row_swap
     e = col_shift - WLON * col_swap
 
+    pl.semaphore_wait(barrier, len(partners))
+
+    halo = []
+    before = slice(0, HALF_COLS)
+    after = slice(HALF_COLS + WLON, 2 * WLON)
+    left_half = slice(0, HALF_COLS)
+    right_half = slice(HALF_COLS, WLON)
+    kept = slice(0, WLAT)
+    borrowed = slice(WLAT, WLAT + HALF_ROWS)
+    for a in range(2):
+        routes = (
+            (inputs[a].at[:, left_half], kept, after, left),
+            (inputs[a].at[:, right_half], kept, before, right),
+            (lat_send.at[a], borrowed, middle, across),
+            (lat_send.at[a, :, left_half], borrowed, after, across_left),
+            (lat_send.at[a, :, right_half], borrowed, before, across_right),
+        )
+        halo.append(
+            [
+                remote(
+                    src,
+                    wides[a].at[rows, columns],
+                    halo_send_sem.at[a, n],
+                    halo_recv_sem.at[a, n],
+                    device,
+                )
+                for n, (src, rows, columns, device) in enumerate(routes)
+            ]
+        )
+    for copies in halo:
+        copies[0].start()
+        copies[1].start()
     loads[0].wait()
     loads[2].wait()
-    for a in range(2):
+    for a, copies in enumerate(halo):
         lat_send[a] = own_block[a, pl.ds(HALF_ROWS * row_swap, HALF_ROWS)]
+        for copy in copies[2:]:
+            copy.start()
+    loads[4].start()
+    loads[5].start()
+    sends = [copy for copies in halo for copy in copies]
 
     load_band.wait()
     k_at = iota((TOK, TOK), 0)
@@ -224,34 +264,6 @@
     allowed = ((k_col < counts) | (k_at == q_at)) & same_side
     bias[...] = jnp.where(allowed, 0.0, -1e30)
 
-    pl.semaphore_wait(barrier, len(partners))
-
-    halo = []
-    before = slice(0, HALF_COLS)
-    after = slice(HALF_COLS + WLON, 2 * WLON)
-    left_half = slice(0, HALF_COLS)
-    right_half = slice(HALF_COLS, WLON)
-    kept = slice(0, WLAT)
-    borrowed = slice(WLAT, WLAT + HALF_ROWS)
-    for a in range(2):
-        copies = []
-        for n, (src, rows, columns, device) in enumerate(
-            (
-                (lat_send.at[a], borrowed, middle, across),
-                (inputs[a].at[:, left_half], kept, after, left),
-                (inputs[a].at[:, right_half], kept, before, right),
-                (lat_send.at[a, :, left_half], borrowed, after, across_left),
-                (lat_send.at[a, :, right_half], borrowed, before, across_right),
-            )
-        ):
-            copy = remote(
-                src, wides[a].at[rows, columns], halo_send_sem.at[a, n], halo_recv_sem.at[a, n], device
-            )
-            copy.start()
-            copies.append(copy)
-        halo.append(copies)
-    sends = [copy for copies in halo for copy in copies]
-
     over_core = []
     over_plane = {}
 
@@ -272,10 +284,8 @@
         over_core.append(copy)
 
     make_window(0)
-    for d in (1, NX - 1) + tuple(range(2, NX - 1)):
+    for d in far_x:
         for axis, peer in ((0, x_peer(d)), (1, y_peer(d))):
-            if (axis, d) in over_plane:
-                continue
             copy = remote(
                 xo.at[core],
                 xg.at[axis, d, core],
@@ -297,8 +307,7 @@
     order = []
     for t in range(2):
         at = slice(t * HEAD_DIM, (t + 1) * HEAD_DIM)
-        for n in range(NX):
-            d = (n + 1) % NX
+        for d in far_x + [0]:
             pair = (wide_at + d) % NX
             lanes = pl.ds(pl.multiple_of(pair * cut, cut), cut)
             order.append((t, at, d, pair, lanes))
@@ -356,7 +365,7 @@
             )
             copy.start()
             over_g[t, d] = copy
-    for d in range(1, NX):
+    for d in far_x:
         copy = remote(
             gall.at[2, (slim_at + d) % NX],
             g_recv.at[2, d],
@@ -386,9 +395,8 @@
         for side, rows in enumerate(sides):
             product = tn(xo[side], own_qk[t, 0] if t < 2 else gall[2, slim_at])
             parts[t, rows] = product.reshape(blocks // 2, own, cut)
-    for d in (1, NX - 1) + tuple(range(2, NX - 1)):
-        if (0, d) not in relays:
-            relay(d)
+    for d in reversed(far_x):
+        relay(d)
     sends += list(relays.values())
 
     gin[1] = grad_in(core)
@@ -412,7 +420,7 @@
     def make_product(t):
         axis = core if t < 2 else 1 - core
         halves = [parts[t, rows].reshape(half, cut) for rows in sides]
-        for d in range(1, NX):
+        for d in reversed(far_x):
             if t == 0:
                 relays[0, d].wait_recv()
                 relays[1, d].wait_recv()
@@ -435,7 +443,7 @@
     for t in range(3):
         make_product(t)
         place = slim_at if t < 2 else wide_at
-        for d in range(1, NX):
+        for d in far_x:
             psend[t, d] = owner_rows(t, (place + d) % NX).astype(BF16)
             copy = remote(
                 psend.at[t, d],
@@ -484,7 +492,7 @@
             over_p[t, d].wait_recv()
             total = total + precv[t, d].astype(F32)
         rz[t] = total.reshape(NZ, NX * own, cut)
-        for d in range(1, NZ):
+        for d in far_z:
             zsend[t, d] = rz[t, (z + d) % NZ].astype(BF16)
             copy = remote(
                 zsend.at[t, d],
@@ -516,7 +524,7 @@
             continue
         group = slice(0, 2) if t == 1 else slice(2, 3)
         place = wide_at if t == 1 else slim_at
-        for d in range(1, NX):
+        for d in far_x:
             copy = remote(
                 rf.at[(place + d) % NX, group],
                 frecv.at[d, group],
@@ -542,6 +550,17 @@
 
     for copy in list(over_z.values()) + list(last.values()):
         copy.wait_send()
+
+
+def write_out(gtok_vmem, gw_vmem, gtok_hbm, gw_hbm, sem):
+    copies = [
+        pltpu.make_async_copy(gtok_vmem, gtok_hbm, sem.at[0]),
+        pltpu.make_async_copy(gw_vmem, gw_hbm, sem.at[1]),
+    ]
+    for copy in copies:
+        copy.start()
+    for copy in copies:
+        copy.wait()
 
 
 def solution(mesh):
@@ -634,6 +653,16 @@
                 )
             )
         )
+        gtok, gw = pl.pallas_call(
+            write_out,
+            out_shape=(
+                jax.ShapeDtypeStruct(gtok.shape, BF16),
+                jax.ShapeDtypeStruct(gw.shape, F32),
+            ),
+            in_specs=[vmem, vmem],
+            out_specs=(hbm, hbm),
+            scratch_shapes=[dma((2,))],
+        )(gtok, gw)
         return gtok.transpose(2, 0, 1, 3), gw
 
     in_specs = (

time: 52 us -> 53.5 us (1.029)
  Pallas kernels: 48.7 us -> 50.2 us
    pallas_call x0 -> x1, Pallas kernels: none -> 1.6 us  [shards(): pl.pallas_call(write_out, out_shape=(jax.ShapeDtypeStruct(gtok.shape, BF1...]
    unnamed x2 -> x4, local copies, waits for them, and re-layouts: 1.28 us -> 1.26 us
where the time goes in v7:
time: 53.5 us; the launch traced here: 53.4 us
  Pallas kernels  50.2 us (94%)
  between operations  1.94 us (4%)
  local copies, waits for them, and re-layouts  1.26 us (2%)
    pallas_call x1, Pallas kernels, shards(): pl.pallas_call(functools.partial(kernel, (n_lon, n_lat, width, half)), ou...  48.6 us
    pallas_call x1, Pallas kernels, shards(): pl.pallas_call(write_out, out_shape=(jax.ShapeDtypeStruct(gtok.shape, BF1...  1.6 us
    unnamed x4, local copies, waits for them, and re-layouts  1.26 us

profile of v7, /device:TPU:1, one launch (start us, length us, event | category | flops | bytes accessed | tf_op | source)
XLA Modules:
  0.0 53.4 jit_solution(16321273720767966342)
XLA Ops:
  1.9 48.6 %shard_map.86 = (bf16[12,6,2,512]{3,2,1,0:T(2,128)(2,1)S(1)}, f32[3,8,512]{2,1,0:T(8,128)S(1)}) custom-call(s32[1]{0:T(128)S(6)} %copy.9.lat_ref, s32[1]{0:T(128)S(6)} %copy.10.lon_ref, s32[24]{0:T(128)} %band_hbm.1, bf16[12,6,2,512]{3,2,1,0:T(2,128)(2,1)} %bitcast.3, bf16[12,6,2,512]{3,2,1,0:T(2,128)(2,1)} %bitcast.4, bf16[3,1024,512]{2,1,0:T(8,128)(2,1)} %wqkv_hbm.1, ...), custom_call_target="tpu_custom_call" | custom-call | tf_op jit(solution)/shard_map/pallas_call | solution.py:579
  50.5 0.0 copy-start
  50.6 0.6 %copy-done = bf16[12,6,2,512]{3,2,1,0:T(2,128)(2,1)} copy-done((bf16[12,6,2,512]{3,2,1,0:T(2,128)(2,1)}, bf16[12,6,2,512]{3,2,1,0:T(2,128)(2,1)S(1)}, u32[]{:S(2)}) %copy-start) | copy-done | bytes 147480
  51.2 0.0 copy-start.1
  51.2 0.6 %copy-done.1 = f32[3,8,512]{2,1,0:T(8,128)} copy-done((f32[3,8,512]{2,1,0:T(8,128)}, f32[3,8,512]{2,1,0:T(8,128)S(1)}, u32[]{:S(2)}) %copy-start.1) | copy-done | bytes 49176
  51.8 1.6 %shard_map.87 = (bf16[12,6,2,512]{3,2,1,0:T(2,128)(2,1)}, f32[3,8,512]{2,1,0:T(8,128)}) custom-call(bf16[12,6,2,512]{3,2,1,0:T(2,128)(2,1)} %copy-done, f32[3,8,512]{2,1,0:T(8,128)} %copy-done.1), custom_call_target="tpu_custom_call" | custom-call | tf_op jit(solution)/shard_map/pallas_call | solution.py:656
Async XLA Ops:
  50.5 0.7 %copy-start = (bf16[12,6,2,512]{3,2,1,0:T(2,128)(2,1)}, bf16[12,6,2,512]{3,2,1,0:T(2,128)(2,1)S(1)}, u32[]{:S(2)}) copy-start(bf16[12,6,2,512]{3,2,1,0:T(2,128)(2,1)S(1)} %get-tuple-element.6.gtok_vmem) | copy-start | bytes 442372
  51.2 0.6 %copy-start.1 = (f32[3,8,512]{2,1,0:T(8,128)}, f32[3,8,512]{2,1,0:T(8,128)S(1)}, u32[]{:S(2)}) copy-start(f32[3,8,512]{2,1,0:T(8,128)S(1)} %get-tuple-element.7.gw_vmem) | copy-start | bytes 147460

commit v8 on v7

--- a/solution.py
+++ b/solution.py
@@ -206,10 +206,10 @@
     pl.semaphore_wait(barrier, len(partners))
 
     halo = []
-    before = slice(0, HALF_COLS)
+    before = slice(1, HALF_COLS)
     after = slice(HALF_COLS + WLON, 2 * WLON)
     left_half = slice(0, HALF_COLS)
-    right_half = slice(HALF_COLS, WLON)
+    right_half = slice(HALF_COLS + 1, WLON)
     kept = slice(0, WLAT)
     borrowed = slice(WLAT, WLAT + HALF_ROWS)
     for a in range(2):
@@ -285,16 +285,16 @@
 
     make_window(0)
     for d in far_x:
-        for axis, peer in ((0, x_peer(d)), (1, y_peer(d))):
+        for role, peer in enumerate((wide_peer(d), slim_peer(d))):
             copy = remote(
                 xo.at[core],
-                xg.at[axis, d, core],
-                xg_send_sem.at[axis, d],
-                xg_recv_sem.at[axis, d],
+                xg.at[role, d, core],
+                xg_send_sem.at[role, d],
+                xg_recv_sem.at[role, d],
                 peer,
             )
             copy.start()
-            over_plane[axis, d] = copy
+            over_plane[role, d] = copy
     sends += list(over_plane.values())
 
     loads[4].wait()
@@ -331,15 +331,17 @@
 
     relays = {}
 
-    def relay(d):
-        for axis in range(2):
-            over_plane[axis, d].wait_recv()
-            mine = xg.at[axis, d, core]
-            copy = remote(
-                mine, mine, relay_send_sem.at[axis, d], relay_recv_sem.at[axis, d], sibling
-            )
-            copy.start()
-            relays[axis, d] = copy
+    def relay(role, d):
+        over_plane[role, d].wait_recv()
+        copy = remote(
+            xg.at[role, d, core],
+            xg.at[1 - role, d, core],
+            relay_send_sem.at[role, d],
+            relay_recv_sem.at[1 - role, d],
+            sibling,
+        )
+        copy.start()
+        relays[1 - role, d] = copy
 
     over_g = {}
     for n, (t, at, d, pair, lanes) in enumerate(order):
@@ -395,8 +397,9 @@
         for side, rows in enumerate(sides):
             product = tn(xo[side], own_qk[t, 0] if t < 2 else gall[2, slim_at])
             parts[t, rows] = product.reshape(blocks // 2, own, cut)
-    for d in reversed(far_x):
-        relay(d)
+    for role in (1, 0):
+        for d in reversed(far_x):
+            relay(role, d)
     sends += list(relays.values())
 
     gin[1] = grad_in(core)
@@ -418,15 +421,14 @@
     over_lat_back.start()
 
     def make_product(t):
-        axis = core if t < 2 else 1 - core
+        role = 0 if t < 2 else 1
         halves = [parts[t, rows].reshape(half, cut) for rows in sides]
         for d in reversed(far_x):
-            if t == 0:
-                relays[0, d].wait_recv()
-                relays[1, d].wait_recv()
+            if t != 1:
+                relays[role, d].wait_recv()
             over_g[t, d].wait_recv()
             for side in range(2):
-                halves[side] = halves[side] + tn(xg[axis, d, side], g_recv[t, d])
+                halves[side] = halves[side] + tn(xg[role, d, side], g_recv[t, d])
         for side, rows in enumerate(sides):
             parts[t, rows] = halves[side].reshape(blocks // 2, own, cut)
 
@@ -550,17 +552,6 @@
 
     for copy in list(over_z.values()) + list(last.values()):
         copy.wait_send()
-
-
-def write_out(gtok_vmem, gw_vmem, gtok_hbm, gw_hbm, sem):
-    copies = [
-        pltpu.make_async_copy(gtok_vmem, gtok_hbm, sem.at[0]),
-        pltpu.make_async_copy(gw_vmem, gw_hbm, sem.at[1]),
-    ]
-    for copy in copies:
-        copy.start()
-    for copy in copies:
-        copy.wait()
 
 
 def solution(mesh):
@@ -653,16 +644,6 @@
                 )
             )
         )
-        gtok, gw = pl.pallas_call(
-            write_out,
-            out_shape=(
-                jax.ShapeDtypeStruct(gtok.shape, BF16),
-                jax.ShapeDtypeStruct(gw.shape, F32),
-            ),
-            in_specs=[vmem, vmem],
-            out_specs=(hbm, hbm),
-            scratch_shapes=[dma((2,))],
-        )(gtok, gw)
         return gtok.transpose(2, 0, 1, 3), gw
 
     in_specs = (

time: 53.5 us -> 51.5 us (0.963)
  the two profiles are of different devices: /device:TPU:1 before, /device:TPU:6 now
where the time goes in v8:
time: 51.5 us; the launch traced here: 51.4 us
  Pallas kernels  48.2 us (94%)
  between operations  1.93 us (4%)
  local copies, waits for them, and re-layouts  1.28 us (2%)
    pallas_call x1, Pallas kernels, shards(): pl.pallas_call(functools.partial(kernel, (n_lon, n_lat, width, half)), ou...  48.2 us
    unnamed x2, local copies, waits for them, and re-layouts  1.28 us

profile of v8, /device:TPU:6, one launch (start us, length us, event | category | flops | bytes accessed | tf_op | source)
XLA Modules:
  0.0 51.4 jit_solution(5484117386894863630)
XLA Ops:
  1.9 48.2 %shard_map.86 = (bf16[12,6,2,512]{3,2,1,0:T(2,128)(2,1)S(1)}, f32[3,8,512]{2,1,0:T(8,128)S(1)}) custom-call(s32[1]{0:T(128)S(6)} %copy.13.lat_ref, s32[1]{0:T(128)S(6)} %copy.14.lon_ref, s32[24]{0:T(128)} %band_hbm.1, bf16[12,6,2,512]{3,2,1,0:T(2,128)(2,1)} %bitcast.4, bf16[12,6,2,512]{3,2,1,0:T(2,128)(2,1)} %bitcast.5, bf16[3,1024,512]{2,1,0:T(8,128)(2,1)} %wqkv_hbm.1, ...), custom_call_target="tpu_custom_call" | custom-call | tf_op jit(solution)/shard_map/pallas_call | solution.py:570
  50.1 0.7 %copy.11 = bf16[2,12,6,512]{3,0,2,1:T(2,128)(2,1)} copy(bf16[2,12,6,512]{3,0,2,1:T(2,128)(2,1)S(1)} %bitcast.3) | data formatting | bytes 294912
  50.8 0.6 %copy.12 = f32[3,8,512]{2,1,0:T(8,128)} copy(f32[3,8,512]{2,1,0:T(8,128)S(1)} %get-tuple-element.7) | data formatting | bytes 98304

commit v9 on v8

--- a/solution.py
+++ b/solution.py
@@ -195,6 +195,8 @@
         load.start()
     loads.append(pltpu.make_async_copy(wqkv_hbm, wqkv, load_sem.at[5]))
     loads.append(pltpu.make_async_copy(wout_hbm, wout, load_sem.at[6]))
+    loads[4].start()
+    loads[5].start()
 
     row_shift = lat_ref[0]
     col_shift = lon_ref[0]
@@ -214,8 +216,8 @@
     borrowed = slice(WLAT, WLAT + HALF_ROWS)
     for a in range(2):
         routes = (
-            (inputs[a].at[:, left_half], kept, after, left),
-            (inputs[a].at[:, right_half], kept, before, right),
+            (own_block.at[a, :, left_half], kept, after, left),
+            (own_block.at[a, :, right_half], kept, before, right),
             (lat_send.at[a], borrowed, middle, across),
             (lat_send.at[a, :, left_half], borrowed, after, across_left),
             (lat_send.at[a, :, right_half], borrowed, before, across_right),
@@ -232,17 +234,15 @@
                 for n, (src, rows, columns, device) in enumerate(routes)
             ]
         )
+    loads[0].wait()
+    loads[2].wait()
     for copies in halo:
         copies[0].start()
         copies[1].start()
-    loads[0].wait()
-    loads[2].wait()
     for a, copies in enumerate(halo):
         lat_send[a] = own_block[a, pl.ds(HALF_ROWS * row_swap, HALF_ROWS)]
         for copy in copies[2:]:
             copy.start()
-    loads[4].start()
-    loads[5].start()
     sends = [copy for copies in halo for copy in copies]
 
     load_band.wait()
@@ -536,6 +536,8 @@
             )
             copy.start()
             last[t, d] = copy
+    for copy in over_z.values():
+        copy.wait_send()
     for d in range(NX):
         if d:
             last[1, d].wait_recv()
@@ -550,7 +552,7 @@
         lanes = pl.ds(pl.multiple_of(((slim_at + NX - d) % NX) * cut, cut), cut)
         gw_ref[2, :, lanes] = values
 
-    for copy in list(over_z.values()) + list(last.values()):
+    for copy in last.values():
         copy.wait_send()
 
 

time: 51.5 us -> 51.2 us (level)
  no operation moved by 1% of the time
where the time goes in v9:
time: 51.2 us; the launch traced here: 51.1 us
  Pallas kernels  47.9 us (94%)
  between operations  1.93 us (4%)
  local copies, waits for them, and re-layouts  1.28 us (2%)
    pallas_call x1, Pallas kernels, shards(): pl.pallas_call(functools.partial(kernel, (n_lon, n_lat, width, half)), ou...  47.9 us
    unnamed x2, local copies, waits for them, and re-layouts  1.28 us

profile of v9, /device:TPU:6, one launch (start us, length us, event | category | flops | bytes accessed | tf_op | source)
XLA Modules:
  0.0 51.1 jit_solution(2425949163835028561)
XLA Ops:
  1.9 47.9 %shard_map.86 = (bf16[12,6,2,512]{3,2,1,0:T(2,128)(2,1)S(1)}, f32[3,8,512]{2,1,0:T(8,128)S(1)}) custom-call(s32[1]{0:T(128)S(6)} %copy.13.lat_ref, s32[1]{0:T(128)S(6)} %copy.14.lon_ref, s32[24]{0:T(128)} %band_hbm.1, bf16[12,6,2,512]{3,2,1,0:T(2,128)(2,1)} %bitcast.4, bf16[12,6,2,512]{3,2,1,0:T(2,128)(2,1)} %bitcast.5, bf16[3,1024,512]{2,1,0:T(8,128)(2,1)} %wqkv_hbm.1, ...), custom_call_target="tpu_custom_call" | custom-call | tf_op jit(solution)/shard_map/pallas_call | solution.py:572
  49.8 0.7 %copy.11 = bf16[2,12,6,512]{3,0,2,1:T(2,128)(2,1)} copy(bf16[2,12,6,512]{3,0,2,1:T(2,128)(2,1)S(1)} %bitcast.3) | data formatting | bytes 294912
  50.5 0.6 %copy.12 = f32[3,8,512]{2,1,0:T(8,128)} copy(f32[3,8,512]{2,1,0:T(8,128)S(1)} %get-tuple-element.7) | data formatting | bytes 98304
